TPU v7x, 32 devices: a whole 2x2x4 slice. The times are simulated.
32 devices in a mesh: dp: 2 (over x), ctx: 4 (over z), tp: 4 (over y, core).
Axes of the slice: x: 2, y: 2, z: 4, core: 2. Of those that a mesh axis runs over, the one named last changes fastest.
Arguments:
- tokens: bfloat16 [2, 2048, 2048], P('dp', ('ctx', 'tp')), may hold values from -6 to 6
- attn_gain: float32 [2048], replicated, may hold values from 0.25 to 1.75
- w_query: bfloat16 [2048, 2048], P(None, 'tp'), may hold values from -0.1875 to 0.1875
- w_key: bfloat16 [2048, 512], P(None, 'tp'), may hold values from -0.1875 to 0.1875
- w_value: bfloat16 [2048, 512], P(None, 'tp'), may hold values from -0.125 to 0.125
- w_out: bfloat16 [2048, 2048], P('tp'), may hold values from -0.75 to 0.75
- ffn_gain: float32 [2048], replicated, may hold values from 0.25 to 1.75
- w_gate: bfloat16 [2048, 8192], P(None, 'tp'), may hold values from -0.125 to 0.125
- w_up: bfloat16 [2048, 8192], P(None, 'tp'), may hold values from -0.125 to 0.125
- w_down: bfloat16 [8192, 2048], P('tp'), may hold values from -0.0625 to 0.0625
- out_cotangent: bfloat16 [2, 2048, 2048], P('dp', ('ctx', 'tp')), may hold values from -6 to 6
- doc_lengths: int32 [2, 8], P('dp'), may hold values from 1 to 1408, as said below
Outputs:
- layer_out: bfloat16 [2, 2048, 2048], P('dp', ('ctx', 'tp'))
- input_grad: float32 [2, 2048, 2048], P('dp', ('ctx', 'tp'))
- grad_attn_gain: float32 [2048], replicated
- grad_w_query: float32 [2048, 2048], P(('dp', 'ctx'), 'tp')
- grad_w_key: float32 [2048, 512], P(('dp', 'ctx'), 'tp')
- grad_w_value: float32 [2048, 512], P(('dp', 'ctx'), 'tp')
- grad_w_out: float32 [2048, 2048], P('tp', ('dp', 'ctx'))
- grad_ffn_gain: float32 [2048], replicated
- grad_w_gate: float32 [2048, 8192], P(('dp', 'ctx'), 'tp')
- grad_w_up: float32 [2048, 8192], P(('dp', 'ctx'), 'tp')
- grad_w_down: float32 [8192, 2048], P('tp', ('dp', 'ctx'))
Inputs may be any that keep to these rules, and one draw needn't show every extreme that they name: `doc_lengths`: each row holds its 8 documents in this order from position 0, then padding. The first has exactly 1408 tokens, the others at least one; together they leave 1 to 255 padding positions.
All inputs are finite; a program needn't handle non-finite values.
Results may differ from a plain program's by a relative error of at most 0.024.
Values may be sent and summed in bfloat16 or wider, within the bound.
No kernel may reach another device: no remote copies, remote signals or barrier semaphores. Data moves between devices by JAX's collectives and lax.ppermute only.
A program may use at most 192 MiB of HBM per device.

v0:
```python
import functools
import math

import jax
import jax.numpy as jnp
import numpy as np
from jax import lax
from jax.experimental import pallas as pl
from jax.experimental.pallas import tpu as pltpu
from jax.sharding import PartitionSpec as P

HD = 64
EPSILON = 1e-05
NEGATIVE = -1e30
ROPE_THETA = 500000.0


def rope_table(head_size):
    base_freq = np.array(
        [ROPE_THETA ** (-2.0 * index / head_size) for index in range(head_size // 2)]
    )
    wavelength = 2.0 * math.pi / base_freq
    blend = (8192.0 / wavelength - 1.0) / 3.0
    middle = (1.0 - blend) * base_freq / 32.0 + blend * base_freq
    return np.where(
        wavelength > 8192.0, base_freq / 32.0, np.where(wavelength < 2048.0, base_freq, middle)
    )


def rms_norm(values_in, gain_vec):
    return (
        values_in
        * lax.rsqrt(jnp.mean(values_in * values_in, axis=-1, keepdims=True) + EPSILON)
        * gain_vec
    )


F32, BF16 = jnp.float32, jnp.bfloat16
VMEM_BYTES = 62 * 1024 * 1024
NN = (((1,), (0,)), ((), ()))
NT = (((1,), (1,)), ((), ()))
TN = (((0,), (0,)), ((), ()))
VMEM = pl.BlockSpec(memory_space=pltpu.VMEM)
SMEM = pl.BlockSpec(memory_space=pltpu.SMEM)
ANYWHERE = pl.BlockSpec(memory_space=pl.ANY)


def dot(left, right, dims=NN):
    return lax.dot_general(left, right, dims, preferred_element_type=F32)


def part_specs(parts, rows, width, col):
    def spec(part):
        if not isinstance(part, tuple):
            return pl.BlockSpec((rows, width), lambda *at: (0, col(*at)))
        j, first = part[1:]
        return pl.BlockSpec(
            (rows, width), lambda *at: (0 if j is None else at[-1][j], first // width + col(*at))
        )

    return [spec(part) for part in parts]


def part_arrays(parts):
    return [part[0] if isinstance(part, tuple) else part for part in parts]


def rows_of(refs):
    return jnp.concatenate([ref[...] for ref in refs], axis=0)


class Chain:
    def __init__(self):
        self.held = []
        self.cost = 58 * 10**8

    def wait(self, *arrays):
        self.held = [*arrays, *self.held]

    def call(
        self, name, body, args, in_specs, out_specs, out_shape, flops, grid=(), scalars=0, scratch=(), zero=False
    ):
        held, count, outs = self.held, len(args), len(out_shape)
        marks, mark_specs = [jax.ShapeDtypeStruct((8, 128), F32)], [ANYWHERE]
        if zero:
            marks.append(jax.ShapeDtypeStruct((1, 1), F32))
            mark_specs.append(SMEM)

        def inner(*refs):
            rest = refs[count + len(held) :]
            given = refs[:scalars] + refs[scalars + len(held) : count + len(held)]
            body(*given, *rest[:outs], *rest[outs + len(marks) :])
            if zero:
                rest[outs + 1][0, 0] = 0.0

        results = pl.pallas_call(
            inner,
            grid_spec=pltpu.PrefetchScalarGridSpec(
                num_scalar_prefetch=scalars,
                grid=grid,
                in_specs=[ANYWHERE] * len(held) + list(in_specs),
                out_specs=[*out_specs, *mark_specs],
                scratch_shapes=list(scratch),
            ),
            out_shape=[*out_shape, *marks],
            compiler_params=pltpu.CompilerParams(
                vmem_limit_bytes=VMEM_BYTES, dimension_semantics=("arbitrary",) * len(grid)
            ),
            cost_estimate=pl.CostEstimate(flops=self.cost, bytes_accessed=1, transcendentals=0),
            name=name,
        )(*args[:scalars], *held, *args[scalars:])
        self.held = [results[outs]]
        if zero:
            self.zero = results[outs + 1][0, 0]
        return results[:outs]


def fill_rows(parts, rows_ref):
    @pl.when(pl.program_id(0) == 0)
    def _():
        rows_ref[...] = rows_of(parts)


def ffn_front_body(count, *refs):
    gate_ref, up_ref, act_ref, slope_ref, silu_ref, rows_ref = refs[count:]
    fill_rows(refs[:count], rows_ref)
    rows = rows_ref[...]
    gate = dot(rows, gate_ref[...])
    up = dot(rows, up_ref[...])
    sigma = 1.0 / (1.0 + jnp.exp(-gate))
    silu = gate * sigma
    act_ref[...] = (silu * up).astype(BF16)
    slope_ref[...] = (up * sigma * (1.0 + gate * (1.0 - sigma))).astype(BF16)
    silu_ref[...] = silu.astype(BF16)


def whole(array):
    return pl.BlockSpec(array.shape, lambda *_: (0,) * array.ndim)


def ffn_front(chain, parts, w_gate, w_up, part=(0, 1), block=512):
    count, width = sum(p.shape[0] for p in parts), parts[0].shape[1]
    units = w_gate.shape[1] // part[1]
    block = min(block, units)
    first = part[0] * (units // block)
    weight = pl.BlockSpec((width, block), lambda j: (0, first + j))
    return chain.call(
        "ffn_front",
        functools.partial(ffn_front_body, len(parts)),
        (*parts, w_gate, w_up),
        [whole(p) for p in parts] + [weight, weight],
        [pl.BlockSpec((count, block), lambda j: (0, j))] * 3,
        [jax.ShapeDtypeStruct((count, units), BF16)] * 3,
        4 * count * width * units,
        grid=(units // block,),
        scratch=[pltpu.VMEM((count, width), BF16)],
        zero=True,
    )


def ffn_back_body(count, perm_ref, *refs):
    down_ref, slope_ref, silu_ref, gate_ref, up_ref, rows_ref = refs[count:]
    fill_rows(refs[:count], rows_ref)
    grad_act = dot(rows_ref[...], down_ref[...], NT)
    gate_ref[...] = (grad_act * slope_ref[...].astype(F32)).astype(BF16)
    up_ref[...] = (grad_act * silu_ref[...].astype(F32)).astype(BF16)


def ffn_back(chain, perm, parts, w_down, slope, silu, block=512):
    count, units = slope.shape
    width = w_down.shape[1]
    block = min(block, units)
    tile = pl.BlockSpec((count, block), lambda j, _: (0, j))
    return chain.call(
        "ffn_back",
        functools.partial(ffn_back_body, len(parts)),
        (perm, *part_arrays(parts), w_down, slope, silu),
        part_specs(parts, count // len(parts), width, lambda *_: 0)
        + [pl.BlockSpec((block, width), lambda j, _: (j, 0)), tile, tile],
        [tile, tile],
        [jax.ShapeDtypeStruct((count, units), BF16)] * 2,
        2 * count * width * units,
        grid=(units // block,),
        scalars=1,
        scratch=[pltpu.VMEM((count, width), BF16)],
    )


def pull_body(count, dims, *refs):
    total = dot(refs[0][...], refs[count][...], dims)
    for i in range(1, count):
        total = total + dot(refs[i][...], refs[count + i][...], dims)
    outs = refs[2 * count :]
    rows = total.shape[0] // len(outs)
    for j, out in enumerate(outs):
        out[...] = total[j * rows : (j + 1) * rows].astype(BF16)


def pull(chain, grads, weights, blocks, dims=NT, block=1024):
    rows, at = grads[0].shape[0], 0 if dims == NT else 1
    width = weights[0].shape[at]
    depth = sum(w.shape[1 - at] for w in weights)
    return chain.call(
        "pull",
        functools.partial(pull_body, len(grads), dims),
        (*grads, *weights),
        [whole(g) for g in grads]
        + [
            pl.BlockSpec((block, w.shape[1]), lambda j: (j, 0))
            if dims == NT
            else pl.BlockSpec((w.shape[0], block), lambda j: (0, j))
            for w in weights
        ],
        [pl.BlockSpec((rows // blocks, block), lambda j: (0, j))] * blocks,
        [jax.ShapeDtypeStruct((rows // blocks, width), BF16)] * blocks,
        2 * rows * width * depth,
        grid=(width // block,),
        zero=True,
    )


def push_body(blocks, perm_ref, rows_ref, weight_ref, out_ref):
    total = dot(rows_ref[...], weight_ref[...]).astype(BF16)
    rows = total.shape[0] // blocks
    for j in range(blocks):
        at = pl.ds(pl.multiple_of(perm_ref[j] * rows, rows), rows)
        out_ref[at] = total[j * rows : (j + 1) * rows]


def push(chain, perm, rows, weight, block=1024):
    count, depth = rows.shape
    width = weight.shape[1]
    return chain.call(
        "push",
        functools.partial(push_body, perm.shape[0]),
        (perm, rows, weight),
        [
            pl.BlockSpec((count, depth), lambda j, _: (0, 0)),
            pl.BlockSpec((depth, block), lambda j, _: (0, j)),
        ],
        [pl.BlockSpec((count, block), lambda j, _: (0, j))],
        [jax.ShapeDtypeStruct((count, width), BF16)],
        2 * count * depth * width,
        grid=(width // block,),
        scalars=1,
    )[0]


def terms_body(count, blocks, scalars, *refs):
    refs = refs[scalars:]
    wide, wide_pair = rows_of(refs[:count]), rows_of(refs[count : 2 * count])
    own, pair = refs[2 * count : 2 * count + 2]
    total = dot(wide, own[...], TN) + dot(wide_pair, pair[...], TN)
    if scalars == 3:
        refs[-1][...] = total.astype(BF16)
        return
    got, sent_ref, left_ref = refs[2 * count + 2 :]
    total = (total + got[...].astype(F32)).astype(BF16)

    @pl.when(pl.program_id(1) < blocks // 2)
    def _():
        sent_ref[...] = total

    @pl.when(pl.program_id(1) >= blocks // 2)
    def _():
        left_ref[...] = total


def weight_terms(chain, perm, wide, wide_pair, cols, cols_pair, narrow, narrow_pair, size, part, received=None, order=None, zero=False):
    tokens, units = narrow.shape
    units //= part[1]
    blocks = cols.shape[0]
    block = units if units <= 2048 else math.gcd(2048, units)
    first = part[0] * (units // block)
    rows = tokens // len(wide)
    units_spec = pl.BlockSpec((tokens, block), lambda j, i, *_: (0, first + j))
    scalars = [cols, cols_pair, perm]
    in_specs = (
        part_specs(wide, rows, size, lambda j, i, *s: s[-3][i])
        + part_specs(wide_pair, rows, size, lambda j, i, *s: s[-2][i])
        + [units_spec, units_spec]
    )
    args = [*part_arrays(wide), *part_arrays(wide_pair), narrow, narrow_pair]
    if received is None:
        out_specs = [pl.BlockSpec((size, block), lambda j, i, *_: (i, j))]
        out = [jax.ShapeDtypeStruct((blocks * size, units), BF16)]
    else:
        half = blocks // 2
        scalars = [order] + scalars
        args.append(received)
        in_specs.append(pl.BlockSpec((size, block), lambda j, i, io, *_: (io[i], j)))
        out_specs = [
            pl.BlockSpec((size, block), lambda j, i, *_: (jnp.minimum(i, half - 1), j)),
            pl.BlockSpec((size, block), lambda j, i, *_: (jnp.maximum(i - half, 0), j)),
        ]
        out = [jax.ShapeDtypeStruct((half * size, units), BF16)] * 2
    return chain.call(
        "weight_terms",
        functools.partial(terms_body, len(wide), blocks, len(scalars)),
        (*scalars, *args),
        in_specs,
        out_specs,
        out,
        4 * tokens * units * blocks * size,
        grid=(units // block, blocks),
        scalars=len(scalars),
        zero=zero or received is not None,
    )


def own_terms_body(count, blocks, scalars, *refs):
    refs = refs[scalars:]
    total = dot(rows_of(refs[:count]), refs[count][...], TN)
    if scalars == 2:
        refs[-1][...] = total.astype(BF16)
        return
    got, sent_ref, left_ref = refs[count + 1 :]
    total = (total + got[...].astype(F32)).astype(BF16)

    @pl.when(pl.program_id(0) < blocks // 2)
    def _():
        sent_ref[...] = total

    @pl.when(pl.program_id(0) >= blocks // 2)
    def _():
        left_ref[...] = total


def own_terms(chain, perm, wide, cols, narrow, size, received=None, order=None):
    tokens, units = narrow.shape
    blocks = cols.shape[0]
    rows = tokens // len(wide)
    half = blocks // 2
    scalars = [cols, perm]
    args = [*part_arrays(wide), narrow]
    in_specs = part_specs(wide, rows, size, lambda i, *s: s[-2][i]) + [whole(narrow)]
    if received is None:
        out_specs = [pl.BlockSpec((size, units), lambda i, *_: (i, 0))]
        out = [jax.ShapeDtypeStruct((blocks * size, units), BF16)]
    else:
        scalars = [order] + scalars
        args.append(received)
        in_specs.append(pl.BlockSpec((size, units), lambda i, io, *_: (io[i], 0)))
        out_specs = [
            pl.BlockSpec((size, units), lambda i, *_: (jnp.minimum(i, half - 1), 0)),
            pl.BlockSpec((size, units), lambda i, *_: (jnp.maximum(i - half, 0), 0)),
        ]
        out = [jax.ShapeDtypeStruct((half * size, units), BF16)] * 2
    return chain.call(
        "own_terms",
        functools.partial(own_terms_body, len(wide), blocks, len(scalars)),
        (*scalars, *args),
        in_specs,
        out_specs,
        out,
        2 * tokens * units * blocks * size,
        grid=(blocks,),
        scalars=len(scalars),
        zero=True,
    )


def halve_body(mine, kept_send, got_send, kept, got, sent_ref, left_ref):
    sent_ref[...] = (kept_send[...].astype(F32) + got_send[...].astype(F32)).astype(BF16)
    left_ref[...] = (kept[...].astype(F32) + got[...].astype(F32)).astype(BF16)


def halve(chain, kept, received, mine, dim):
    steps = math.gcd(4, kept.shape[1 - dim] // 128)
    shape = list(kept.shape)
    shape[dim] //= 2
    block = list(shape)
    block[1 - dim] //= steps

    def spec(flip_half):
        def at(j, m):
            half = 1 - m[0] if flip_half else m[0]
            return (half, j) if dim == 0 else (j, half)

        return pl.BlockSpec(tuple(block), at)

    out_spec = pl.BlockSpec(tuple(block), lambda j, m: (0, j) if dim == 0 else (j, 0))
    out = jax.ShapeDtypeStruct(tuple(shape), BF16)
    return chain.call(
        "halve",
        halve_body,
        (mine, kept, received, kept, received),
        [spec(True), spec(True), spec(False), spec(False)],
        [out_spec, out_spec],
        [out, out],
        kept.size,
        grid=(steps,),
        scalars=1,
        zero=True,
    )


def swap_halves(values_in):
    half = HD // 2
    width = values_in.shape[1]
    if width % 128:
        parts = []
        for at in range(0, width, HD):
            parts += [values_in[:, at + half : at + HD], values_in[:, at : at + half]]
        return jnp.concatenate(parts, axis=1)
    lane = lax.broadcasted_iota(jnp.int32, values_in.shape, 1)
    return jnp.where(
        lane % HD < half,
        pltpu.roll(values_in, width - half, 1),
        pltpu.roll(values_in, half, 1),
    )


def turn(values_in, cos_ref, sin_ref, sign):
    count = values_in.shape[1] // HD
    cos = jnp.concatenate([cos_ref[...]] * count, axis=1)
    sin = jnp.concatenate([sin_ref[...]] * count, axis=1)
    return values_in * cos + sign * (swap_halves(values_in) * sin)


def project_body(count, *refs):
    q_ref, k_ref, v_ref, cos_ref, sin_ref, kv_ref, query_ref = refs[count:]
    rows = rows_of(refs[:count])
    width = k_ref.shape[1]
    kv_ref[:, :width] = turn(dot(rows, k_ref[...]), cos_ref, sin_ref, 1.0).astype(BF16)
    kv_ref[:, width:] = dot(rows, v_ref[...]).astype(BF16)
    queries = turn(dot(rows, q_ref[...]), cos_ref, sin_ref, 1.0).astype(BF16)
    query_ref[...] = (queries.astype(F32) * (1.0 / math.sqrt(HD))).astype(BF16)


def project(chain, parts, w_query, w_key, w_value, cos, sin):
    count = sum(p.shape[0] for p in parts)
    kv = jax.ShapeDtypeStruct((count, 2 * w_key.shape[1]), BF16)
    query = jax.ShapeDtypeStruct((count, w_query.shape[1]), BF16)
    return chain.call(
        "project",
        functools.partial(project_body, len(parts)),
        (*parts, w_query, w_key, w_value, cos, sin),
        [VMEM] * (len(parts) + 5),
        [VMEM] * 2,
        [kv, query],
        2 * count * parts[0].shape[1] * (query.shape[1] + kv.shape[1]),
    )


def half_piece(places_ref, half, halves):
    top = places_ref[2] // halves
    return jnp.where(top == half, places_ref[0], 2 * places_ref[1] - 1 - places_ref[0])


def doc_start(places_ref, docs, position):
    end = 0
    start = position * 0
    for i in range(docs):
        end = end + places_ref[4 + i]
        start = jnp.where(position >= end, end, start)
    return start, position < end


def positions_of(places_ref, piece, halves, rows, shape, dim):
    row = lax.broadcasted_iota(jnp.int32, shape, dim)
    inner = lax.rem(places_ref[2], halves) * places_ref[3]
    return piece * rows + (row ^ inner)


def tile_count(tiles, rows):
    return sum(t.shape[0] for t in tiles) // rows + 2


def half_of(places_ref, docs, halves, half, rows, group):
    piece = half_piece(places_ref, half, halves)
    position = positions_of(places_ref, piece, halves, rows, (1, rows), 1)
    start, valid = doc_start(places_ref, docs, position)
    first = doc_start(places_ref, docs, piece * rows)[0]
    position, start, valid = (
        jnp.concatenate([v] * group, axis=1) for v in (position, start, valid.astype(jnp.int32))
    )
    return piece, position, start, valid, first


def tile_piece(places_ref, docs, halves, t):
    given = places_ref[4 + docs + jnp.maximum(t - 2, 0)]
    own = jnp.where(t == 0, half_piece(places_ref, 0, halves), half_piece(places_ref, 1, halves))
    return jnp.where(t < 2, own, given)


def split_tiles(kv_refs, rows, keys_ref, values_ref, ones):
    kv_heads = keys_ref.shape[0]
    t = 0
    for ref in kv_refs:
        for row in range(0, ref.shape[0], rows):
            for g in range(kv_heads):
                keys_ref[g, t] = ref[row : row + rows, g * HD : (g + 1) * HD]
                values = ref[row : row + rows, (kv_heads + g) * HD : (kv_heads + g + 1) * HD]
                if ones:
                    values = jnp.concatenate([values, jnp.ones_like(values)], axis=1)
                values_ref[g, t] = values
            t += 1


def split_heads(ref, rows, group, out_ref, change=lambda v, half: v):
    kv_heads = out_ref.shape[0] // 2
    for half in range(2):
        for g in range(kv_heads):
            for i in range(group):
                head = (g * group + i) * HD
                values = ref[half * rows : (half + 1) * rows, head : head + HD]
                out_ref[half * kv_heads + g, i * rows : (i + 1) * rows] = change(values, half)


def attend_body(docs, halves, count, places_ref, q_ref, kv_ref, *refs):
    tile_refs, (merged_ref, total_ref) = refs[:count], refs[count : count + 2]
    keys_ref, values_ref, stack_ref, scores_ref, peak_ref, sums_ref, out_ref = refs[count + 2 :]
    rows = q_ref.shape[0] // 2
    kv_heads, tiles = keys_ref.shape[:2]
    group = q_ref.shape[1] // HD // kv_heads
    split_tiles([kv_ref, *tile_refs], rows, keys_ref, values_ref, True)
    split_heads(q_ref, rows, group, stack_ref)

    def one(hg, carry):
        half, g = hg // kv_heads, hg % kv_heads
        q_piece, q_pos, q_start, valid, first = half_of(places_ref, docs, halves, half, rows, group)
        peak_ref[...] = jnp.full(peak_ref.shape, NEGATIVE, F32)
        sums_ref[...] = jnp.zeros(sums_ref.shape, F32)

        def score(t, carry):
            piece = tile_piece(places_ref, docs, halves, t)

            @pl.when((piece <= q_piece) & ((piece + 1) * rows > first))
            def _():
                k_pos = positions_of(places_ref, piece, halves, rows, (rows, 1), 0)
                scores = dot(keys_ref[g, t], stack_ref[hg], NT)
                scores = jnp.where((k_pos <= q_pos) & (k_pos >= q_start), scores, NEGATIVE)
                scores_ref[t] = scores
                top = jnp.max(scores.reshape(rows // 8, 8, group * rows), axis=0)
                peak_ref[...] = jnp.maximum(peak_ref[...], top)

            return carry

        lax.fori_loop(0, tiles, score, 0)
        peak = jnp.max(peak_ref[...], axis=0, keepdims=True)

        def weigh(t, carry):
            piece = tile_piece(places_ref, docs, halves, t)

            @pl.when((piece <= q_piece) & ((piece + 1) * rows > first))
            def _():
                expo = jnp.exp(scores_ref[t] - peak).astype(BF16)
                sums_ref[...] += dot(values_ref[g, t], expo, TN)

            return carry

        lax.fori_loop(0, tiles, weigh, 0)
        total = sums_ref[HD : HD + 1]
        out_ref[hg] = jnp.where(valid > 0, sums_ref[...] / total, 0.0).T.astype(BF16)
        total_ref[hg] = peak + jnp.log(total)
        return carry

    lax.fori_loop(0, 2 * kv_heads, one, 0)
    for half in range(2):
        for g in range(kv_heads):
            for i in range(group):
                head = (g * group + i) * HD
                merged_ref[half * rows : (half + 1) * rows, head : head + HD] = out_ref[
                    half * kv_heads + g, i * rows : (i + 1) * rows, :HD
                ]


def attend(chain, places, docs, halves, query, kv, tiles):
    tokens, width = query.shape
    rows = tokens // 2
    heads, kv_heads = width // HD, kv.shape[1] // 2 // HD
    span = heads // kv_heads * rows
    tile_num = tile_count(tiles, rows)
    return chain.call(
        "attend",
        functools.partial(attend_body, docs, halves, len(tiles)),
        (places, query, kv, *tiles),
        [SMEM] + [VMEM] * (2 + len(tiles)),
        [VMEM] * 2,
        [
            jax.ShapeDtypeStruct((tokens, width), BF16),
            jax.ShapeDtypeStruct((2 * kv_heads, 1, span), F32),
        ],
        8 * tokens * rows * tile_num * width,
        scratch=[
            pltpu.VMEM((kv_heads, tile_num, rows, HD), BF16),
            pltpu.VMEM((kv_heads, tile_num, rows, 2 * HD), BF16),
            pltpu.VMEM((2 * kv_heads, span, HD), BF16),
            pltpu.VMEM((tile_num, rows, span), F32),
            pltpu.VMEM((8, span), F32),
            pltpu.VMEM((2 * HD, span), F32),
            pltpu.VMEM((2 * kv_heads, span, 2 * HD), BF16),
        ],
    )


def attend_back_body(docs, halves, count, parts, *refs):
    places_ref, q_ref, merged_ref, total_ref, cos_ref, sin_ref, w_ref = refs[:7]
    kv_ref, tile_refs = refs[7 + parts], refs[8 + parts : 8 + parts + count]
    grad_q_ref, grad_own_ref, *grad_tile_refs = refs[8 + parts + count : 10 + parts + 2 * count]
    grad_ref, keys_ref, values_ref, stack_ref, grads_ref, outs_ref, q_sum_ref, kv_sum_ref = refs[
        10 + parts + 2 * count :
    ]
    rows = q_ref.shape[0] // 2
    kv_heads, tiles = keys_ref.shape[:2]
    group = q_ref.shape[1] // HD // kv_heads
    grad_ref[...] = dot(rows_of(refs[7 : 7 + parts]), w_ref[...], NT).astype(BF16)
    split_tiles([kv_ref, *tile_refs], rows, keys_ref, values_ref, False)
    split_heads(q_ref, rows, group, stack_ref)
    split_heads(merged_ref, rows, group, outs_ref)
    shown = []
    for half in range(2):
        piece = half_piece(places_ref, half, halves)
        position = positions_of(places_ref, piece, halves, rows, (rows, 1), 0)
        shown.append(doc_start(places_ref, docs, position)[1])

    def masked(values, half):
        return jnp.where(shown[half], values.astype(F32), 0.0).astype(BF16)

    split_heads(grad_ref, rows, group, grads_ref, masked)
    kv_sum_ref[...] = jnp.zeros(kv_sum_ref.shape, F32)
    q_sum_ref[...] = jnp.zeros(q_sum_ref.shape, F32)

    def one(hg, carry):
        half, g = hg // kv_heads, hg % kv_heads
        q_piece, q_pos, q_start, _, first = half_of(places_ref, docs, halves, half, rows, group)
        product = grads_ref[hg].astype(F32) * outs_ref[hg].astype(F32)
        high = product.astype(BF16)
        low = (product - high.astype(F32)).astype(BF16)
        ones = jnp.ones((8, HD), BF16)
        delta = (dot(ones, high, NT) + dot(ones, low, NT))[:1]
        totals = total_ref[hg]

        def back(t, carry):
            piece = tile_piece(places_ref, docs, halves, t)

            @pl.when((piece <= q_piece) & ((piece + 1) * rows > first))
            def _():
                k_pos = positions_of(places_ref, piece, halves, rows, (rows, 1), 0)
                keys, queries, grads = keys_ref[g, t], stack_ref[hg], grads_ref[hg]
                scores = dot(keys, queries, NT) - totals
                scores = jnp.where((k_pos <= q_pos) & (k_pos >= q_start), scores, NEGATIVE)
                probs = jnp.exp(scores)
                grad_probs = dot(values_ref[g, t], grads, NT)
                grad_scores = (probs * (grad_probs - delta)).astype(BF16)
                q_sum_ref[hg, :HD] += dot(keys, grad_scores, TN)
                kv_sum_ref[t, 0, g] += dot(grad_scores, queries)
                kv_sum_ref[t, 1, g] += dot(probs.astype(BF16), grads)

            return carry

        lax.fori_loop(0, tiles, back, 0)
        return carry

    lax.fori_loop(0, 2 * kv_heads, one, 0)
    for half in range(2):
        at = pl.ds(half * rows, rows)
        for g in range(kv_heads):
            q_sum = q_sum_ref[half * kv_heads + g].T
            for i in range(group):
                head = (g * group + i) * HD
                part = q_sum[i * rows : (i + 1) * rows, :HD] * (1.0 / math.sqrt(HD))
                part = part * cos_ref[at] - swap_halves(part) * sin_ref[at]
                grad_q_ref[at, head : head + HD] = part.astype(BF16)
    targets = [
        (out, row) for out in (grad_own_ref, *grad_tile_refs) for row in range(0, out.shape[0], rows)
    ]
    for t, (out_ref, row) in enumerate(targets):
        for part in range(2):
            for g in range(kv_heads):
                cols = slice((part * kv_heads + g) * HD, (part * kv_heads + g + 1) * HD)
                out_ref[row : row + rows, cols] = kv_sum_ref[t, part, g].astype(out_ref.dtype)


def attend_back(chain, places, docs, halves, query, merged, totals, cos, sin, w_out, grads, kv, tiles):
    tokens, width = query.shape
    rows = tokens // 2
    kv_heads = kv.shape[1] // 2 // HD
    span = width // HD // kv_heads * rows
    tile_num = tile_count(tiles, rows)
    stack = pltpu.VMEM((2 * kv_heads, span, HD), BF16)
    return chain.call(
        "attend_back",
        functools.partial(attend_back_body, docs, halves, len(tiles), len(grads)),
        (places, query, merged, totals, cos, sin, w_out, *grads, kv, *tiles),
        [SMEM] + [VMEM] * (7 + len(grads) + len(tiles)),
        [VMEM] * (2 + len(tiles)),
        [jax.ShapeDtypeStruct((tokens, width), BF16), jax.ShapeDtypeStruct(kv.shape, F32)]
        + [jax.ShapeDtypeStruct(t.shape, BF16) for t in tiles],
        16 * tokens * rows * tile_num * width,
        scratch=[
            pltpu.VMEM((tokens, width), BF16),
            pltpu.VMEM((kv_heads, tile_num, rows, HD), BF16),
            pltpu.VMEM((kv_heads, tile_num, rows, HD), BF16),
            stack,
            stack,
            stack,
            pltpu.VMEM((2 * kv_heads, 2 * HD, span), F32),
            pltpu.VMEM((tile_num, 2, kv_heads, rows, HD), F32),
        ],
    )


def finish_body(starts_ref, cos_ref, sin_ref, query_ref, own_ref, *refs):
    parts, (all_ref, key_ref, value_ref, total_ref) = refs[:-4], refs[-4:]
    total_ref[...] = own_ref[...]
    rows = own_ref.shape[0] // 2
    tiles = [(part, row) for part in parts for row in range(0, part.shape[0], rows)]
    for t, (part, row) in enumerate(tiles):
        at = pl.ds(pl.multiple_of(starts_ref[t] * rows, rows), rows)
        total_ref[at] += part[row : row + rows].astype(F32)
    width = key_ref.shape[1]
    keys = turn(total_ref[:, :width], cos_ref, sin_ref, -1.0).astype(BF16)
    values = total_ref[:, width:].astype(BF16)
    key_ref[...] = keys
    value_ref[...] = values
    wide = query_ref.shape[1]
    all_ref[:, :wide] = query_ref[...]
    all_ref[:, wide : wide + width] = keys
    all_ref[:, wide + width :] = values


def finish(chain, starts, cos, sin, grad_query, own, parts):
    tokens, width = own.shape
    wide = grad_query.shape[1] + width
    one = jax.ShapeDtypeStruct((tokens, width // 2), BF16)
    return chain.call(
        "finish",
        finish_body,
        (starts, cos, sin, grad_query, own, *parts),
        [SMEM] + [VMEM] * (4 + len(parts)),
        [VMEM] * 3,
        [jax.ShapeDtypeStruct((tokens, wide), BF16), one, one],
        20 * tokens * width,
        scratch=[pltpu.VMEM((tokens, width), F32)],
    )


def flip(values_in, axis, mask):
    count = lax.axis_size(axis)
    return lax.ppermute(values_in, axis, [(i, i ^ mask) for i in range(count)])


def later(values_in, zero):
    return (values_in.astype(F32) + zero).astype(BF16)


def tp_gather(shard, zero=None):
    count = lax.axis_size("tp")
    parts = {0: shard}
    mask = 2
    while mask < count:
        parts.update({j ^ mask: flip(part, "tp", mask) for j, part in parts.items()})
        mask *= 2
    for j, part in list(parts.items()):
        parts[j ^ 1] = flip(later(part, zero) if j and zero is not None else part, "tp", 1)
    return [parts[j] for j in range(count)]


def tp_scatter(terms):
    count = len(terms)
    received = {j: flip(terms[j + 1], "tp", 1) for j in reversed(range(0, count, 2))}
    blocks = {j: terms[j].astype(F32) + part.astype(F32) for j, part in received.items()}
    mask = count // 2
    while mask > 2:
        for j in range(0, mask, 2):
            blocks[j] = blocks[j] + flip(blocks[j + mask].astype(BF16), "tp", mask).astype(F32)
        mask //= 2
    sent = blocks[2].astype(BF16)
    return sent, lambda: blocks[0] + flip(sent, "tp", 2).astype(F32)


def sum_over(values_in, axis):
    mask = 1
    while mask < lax.axis_size(axis):
        values_in = values_in + flip(values_in, axis, mask)
        mask *= 2
    return values_in


def tile_plan(count):
    ends = 2 * count + 3
    needed = []
    for c in range(count):
        pieces = set()
        for held in (c, 2 * count - 1 - c):
            first = ends // 2 if 2 * held >= ends else 0
            pieces |= set(range(first, held + 1))
        needed.append(pieces - {c, 2 * count - 1 - c})
    plan = []
    for k in range(1, count):
        chosen = {}
        for c in range(count):
            source = (c + k) % count
            pieces = sorted(needed[c] & {source, 2 * count - 1 - source})
            if pieces:
                chosen[source] = (c, pieces)
        if chosen:
            plan.append(([(s, c) for s, (c, _) in chosen.items()], {s: p for s, (_, p) in chosen.items()}))
    return plan


def other_columns(values_in, pick_odd, size):
    blocks = values_in.shape[1] // size
    even, odd = (
        jnp.concatenate([values_in[:, b * size : (b + 1) * size] for b in range(at, blocks, 2)], axis=1)
        for at in (0, 1)
    )
    return jnp.where(pick_odd, odd, even)


def per_device(
    tokens,
    attn_gain,
    w_query,
    w_key,
    w_value,
    w_out,
    ffn_gain,
    w_gate,
    w_up,
    w_down,
    out_cotangent,
    doc_lengths,
):
    ctx_count, ctx_rank = lax.axis_size("ctx"), lax.axis_index("ctx")
    dp_count, dp_rank = lax.axis_size("dp"), lax.axis_index("dp")
    tp_count, tp_rank = lax.axis_size("tp"), lax.axis_index("tp")
    tp_rows, width = tokens.shape[1:]
    ctx_rows = tp_rows * tp_count
    near_rows = ctx_rows // 2
    halves = tp_count // 2
    docs = doc_lengths.shape[1]
    size = width // (dp_count * ctx_count)
    chain = Chain()

    plan = tile_plan(ctx_count)
    nowhere = 2 * ctx_count
    widths = [max(len(p) for p in pieces.values()) for _, pieces in plan]
    got = np.full((ctx_count, sum(widths)), nowhere, np.int32)
    gave = np.zeros((ctx_count, sum(widths)), np.int32)
    for t, (moves, pieces) in enumerate(plan):
        first = sum(widths[:t])
        for source, target in moves:
            listed = pieces[source]
            got[target, first : first + len(listed)] = listed
            high = int(listed[0] != source)
            gave[source, first : first + widths[t]] = [high, 1 - high][: widths[t]]
    top = tp_rank // halves
    starts = jnp.asarray(gave)[ctx_rank] ^ top
    here = jnp.stack([ctx_rank, jnp.int32(ctx_count), tp_rank, jnp.int32(tp_rows)])
    places = jnp.concatenate([here, doc_lengths[0], jnp.asarray(got)[ctx_rank]]).astype(jnp.int32)

    within = jnp.arange(ctx_rows, dtype=jnp.int32) ^ (tp_rank * tp_rows)
    piece = jnp.where(within < near_rows, ctx_rank, 2 * ctx_count - 1 - ctx_rank)
    position = (piece * near_rows + within % near_rows).astype(F32)
    inv_freq = jnp.asarray(rope_table(HD), F32)
    angles = position[:, None] * inv_freq[None, :]
    cosine, sine = jnp.cos(angles), jnp.sin(angles)
    cos = jnp.concatenate([cosine, cosine], axis=1)
    sin = jnp.concatenate([-sine, sine], axis=1)

    perm = jnp.arange(tp_count, dtype=jnp.int32) ^ tp_rank
    mine = ctx_rank % 2
    pairs = ctx_count // 2
    steps = jnp.arange(pairs, dtype=jnp.int32)

    def cols_of(dp_index):
        return (dp_index * ctx_count + 2 * steps + mine).astype(jnp.int32)

    def packed_cols_of(dp_index):
        return (dp_index * pairs + steps).astype(jnp.int32)

    bit = ctx_rank // pairs % 2
    order = ((1 - bit) * (pairs // 2) + steps) % pairs

    class WeightGrad:
        def __init__(self, wide, wide_pair, packed, narrow, narrow_pair, part=(0, 1)):
            def terms(dp_index, *received, zero=False):
                cols = cols_of(dp_index)
                cols_pair = packed_cols_of(dp_index) if packed else cols
                if received:
                    cols, cols_pair = cols[order], cols_pair[order]
                return weight_terms(
                    chain, perm, wide, wide_pair, cols, cols_pair, narrow, narrow_pair, size, part, *received, zero=zero
                )

            self.terms = terms

        def send(self, zero=False):
            self.sent = self.terms(1 - dp_rank, zero=zero)[0]
            self.received = flip(self.sent, "dp", 1)
            return self

        def keep(self):
            chain.wait(self.received)
            sent, self.kept = self.terms(dp_rank, self.received, order)
            self.received = flip(sent, "ctx", pairs)
            self.spread(pairs // 2)

        def spread(self, mask):
            while mask > 1:
                half = jnp.reshape(ctx_rank // mask % 2, (1,))
                sent, self.kept = halve(chain, self.kept, self.received, half, 0)
                self.received = flip(sent, "ctx", mask)
                mask //= 2

        def total(self, zero):
            return (self.kept.astype(F32) + zero) + self.received.astype(F32)

    class OutGrad(WeightGrad):
        def __init__(self, wide, narrow):
            self.wide, self.narrow = wide, narrow

        def pair(self):
            both = jnp.concatenate([steps, steps + pairs])
            cols = (2 * both + 1 - mine).astype(jnp.int32)
            self.received = flip(own_terms(chain, perm, self.wide, cols, self.narrow, size)[0], "ctx", 1)

        def send(self):
            half = ((1 - dp_rank) * pairs + steps).astype(jnp.int32)
            order = jnp.concatenate([half, (dp_rank * pairs + steps).astype(jnp.int32)])
            chain.wait(self.received)
            sent, self.kept = own_terms(
                chain, perm, self.wide, 2 * order + mine, self.narrow, size, self.received, order
            )
            self.received = flip(sent, "dp", 1)

        def keep(self):
            chain.wait(self.received)
            self.spread(pairs)

    inputs = tokens[0].astype(F32)
    normed_local = rms_norm(inputs, attn_gain).astype(BF16)
    normed = tp_gather(normed_local)
    grad_fb_local = out_cotangent[0]
    from_pair = flip(
        jnp.concatenate([grad_fb_local, other_columns(normed_local, mine == 0, size)], axis=1), "ctx", 1
    )
    gathered = lax.all_gather(
        jnp.concatenate([grad_fb_local, from_pair], axis=1), "tp", axis=0, tiled=True
    )
    grad_fb, grad_fb_pair, normed_pair = (
        [(gathered, j, first) for j in range(tp_count)] for first in (0, width, 2 * width)
    )
    kv, query = project(chain, normed, w_query, w_key, w_value, cos, sin)
    low_half = lax.dynamic_slice_in_dim(kv, top * near_rows, near_rows, 0)
    high_half = lax.dynamic_slice_in_dim(kv, (1 - top) * near_rows, near_rows, 0)
    tiles = []
    for t, (moves, _) in enumerate(plan):
        low_first = jnp.asarray(gave)[ctx_rank, sum(widths[:t])] == 0
        held = [jnp.where(low_first, low_half, high_half), jnp.where(low_first, high_half, low_half)]
        held = jnp.concatenate(held[: widths[t]], axis=0)
        tiles.append(lax.ppermute(held, "ctx", moves))
    chain.wait(*tiles)
    merged, totals = attend(chain, places, docs, halves, query, kv, tiles)
    out_terms = pull(chain, [merged], [w_out], tp_count, NN)
    hidden_state = inputs + tp_scatter(out_terms)[1]()

    normed_ffn_local = rms_norm(hidden_state, ffn_gain).astype(BF16)
    normed_ffn = tp_gather(normed_ffn_local)
    act, slope, silu = ffn_front(chain, normed_ffn, w_gate, w_up)
    normed_ffn_pair = tp_gather(flip(normed_ffn_local, "ctx", 1), chain.zero)
    act_pair, slope_pair, silu_pair = ffn_front(chain, normed_ffn_pair, w_gate, w_up)

    down_w = WeightGrad(grad_fb, grad_fb_pair, False, act, act_pair).send()
    grad_gate, grad_up = ffn_back(chain, perm, grad_fb, w_down, slope, silu)
    nffn_terms = pull(chain, [grad_gate, grad_up], [w_gate, w_up], tp_count)
    nffn_sent, nffn_sum = tp_scatter(nffn_terms)
    grad_gate_pair, grad_up_pair = ffn_back(chain, perm, grad_fb_pair, w_down, slope_pair, silu_pair)
    chain.wait(nffn_sent)
    gate_w = WeightGrad(normed_ffn, normed_ffn_pair, False, grad_gate, grad_gate_pair).send()
    up_w = WeightGrad(normed_ffn, normed_ffn_pair, False, grad_up, grad_up_pair)
    down_w.keep()
    grad_nffn = nffn_sum() + chain.zero
    grad_state_norm, grad_ffn_gain = jax.vjp(rms_norm, hidden_state, ffn_gain)[1](grad_nffn)
    grad_state = grad_fb_local.astype(F32) + grad_state_norm
    grad_sb_local = grad_state.astype(BF16)
    grad_sb = tp_gather(grad_sb_local)
    chain.wait(grad_sb_local)
    up_w.send()

    grad_query, own, *sent = attend_back(
        chain, places, docs, halves, query, merged, totals, cos, sin, w_out, grad_sb, kv, tiles
    )
    returned = [
        lax.ppermute(part, "ctx", [(target, source) for source, target in moves])
        for part, (moves, _) in zip(sent, plan)
    ]
    chain.wait(down_w.received)
    gate_w.keep()
    chain.wait(*returned)
    grad_qkv, grad_key, grad_value = finish(chain, starts, cos, sin, grad_query, own, returned)
    grad_qkv_pair = flip(grad_qkv, "ctx", 1)
    up_w.keep()
    out_w = OutGrad(grad_sb, merged)
    out_w.pair()
    back_terms = pull(chain, [grad_query, grad_key, grad_value], [w_query, w_key, w_value], tp_count)
    layer_terms = push(chain, perm, act, w_down)
    layer_sum = lax.psum_scatter(layer_terms, "tp", scatter_dimension=0, tiled=True)
    layer_out = (hidden_state + layer_sum.astype(F32)).astype(BF16)
    normed_sent, normed_sum = tp_scatter(back_terms)
    chain.wait(grad_qkv_pair)
    qkv_w = WeightGrad(normed, normed_pair, True, grad_qkv, grad_qkv_pair).send(True)
    grad_normed = normed_sum() + chain.zero
    grad_input_norm, grad_attn_gain = jax.vjp(rms_norm, inputs, attn_gain)[1](grad_normed)
    input_grad = grad_state + grad_input_norm
    sent_zero = chain.zero
    chain.wait(gate_w.received)
    qkv_w.keep()
    out_w.send()
    out_zero = chain.zero
    chain.wait(up_w.received)
    out_w.keep()
    zero = chain.zero
    gains = sum_over(jnp.stack([grad_attn_gain, grad_ffn_gain]) + out_zero, "tp")
    gains = sum_over(sum_over(gains + zero, "dp"), "ctx")
    q_width, kv_width = w_query.shape[1], w_key.shape[1]
    out_total = out_w.total(zero).T
    qkv_total = qkv_w.total(zero)
    return (
        layer_out[None],
        input_grad[None],
        gains[0],
        qkv_total[:, :q_width],
        qkv_total[:, q_width : q_width + kv_width],
        qkv_total[:, q_width + kv_width :],
        out_total,
        gains[1],
        gate_w.total(out_zero),
        up_w.total(zero),
        down_w.total(sent_zero).T,
    )


def solution(mesh):
    placed = (
        P("dp", ("ctx", "tp"), None),
        P(),
        P(None, "tp"),
        P(None, "tp"),
        P(None, "tp"),
        P("tp", None),
        P(),
        P(None, "tp"),
        P(None, "tp"),
        P("tp", None),
        P("dp", ("ctx", "tp"), None),
        P("dp", None),
    )
    return jax.shard_map(
        per_device,
        mesh=mesh,
        in_specs=placed,
        out_specs=(
            P("dp", ("ctx", "tp"), None),
            P("dp", ("ctx", "tp"), None),
            P(),
            P(("dp", "ctx"), "tp"),
            P(("dp", "ctx"), "tp"),
            P(("dp", "ctx"), "tp"),
            P("tp", ("dp", "ctx")),
            P(),
            P(("dp", "ctx"), "tp"),
            P(("dp", "ctx"), "tp"),
            P("tp", ("dp", "ctx")),
        ),
        check_vma=False,
    )
```

profile of v0, /device:TPU:0, one launch (start us, length us, event | category | flops | bytes accessed | tf_op | source)
XLA Modules:
  0.0 432.6 jit_solution(9521458398806680149)
XLA Ops:
  17.0 10.8 %collective-permute-done.1.refs_2_.refs_7_.refs_9_ = bf16[128,2048]{1,0:T(8,128)(2,1)S(1)} collective-permute-done((bf16[128,2048]{1,0:T(8,128)(2,1)S(1)}, bf16[128,2048]{1,0:T(8,128)(2,1)S(1)}, u32[]{:S(2)}, u32[]{:S(2)}) %collective-permute-start.1) | collective-permute-done | bytes 524320 | tf_op jit(solution)/shard_map/ppermute | solution.py:742
  39.8 6.5 %project.1 = (bf16[512,256]{1,0:T(8,128)(2,1)}, bf16[512,512]{1,0:T(8,128)(2,1)}, f32[8,128]{1,0:T(8,128)}) custom-call(bf16[128,2048]{1,0:T(8,128)(2,1)} %copy-done.1, bf16[128,2048]{1,0:T(8,128)(2,1)} %copy-done.5, bf16[128,2048]{1,0:T(8,128)(2,1)} %copy-done.4, bf16[128,2048]{1,0:T(8,128)(2,1)} %copy-done.6, bf16[2048,512]{1,0:T(8,128)(2,1)} %refs_4_.5, ...), custom_call_target="tpu_custom_call" | custom-call | flops 5800000000 | bytes 1 | tf_op jit(solution)/shard_map/project/pallas_call | solution.py:96
  62.3 8.8 %attend.1 = (bf16[512,512]{1,0:T(8,128)(2,1)}, f32[4,1,1024]{2,1,0:T(1,128)}, f32[8,128]{1,0:T(8,128)}) custom-call(bf16[512,256]{1,0:T(8,128)(2,1)} %copy-done.25, bf16[256,256]{1,0:T(8,128)(2,1)} %copy-done.28, bf16[256,256]{1,0:T(8,128)(2,1)} %copy-done.27, f32[8,128]{1,0:T(8,128)} %get-tuple-element.91.refs_3_, s32[16]{0:T(128)} %concatenate.33.refs_4_.refs_1_, ...), custom_call_target="tpu_custom_call" | custom-call | flops 5800000000 | bytes 1 | tf_op jit(solution)/shard_map/attend/pallas_call | solution.py:96
  79.8 12.5 %collective-permute-done.8 = bf16[128,2048]{1,0:T(8,128)(2,1)S(1)} collective-permute-done((bf16[128,2048]{1,0:T(8,128)(2,1)S(1)}, bf16[128,2048]{1,0:T(8,128)(2,1)S(1)}, u32[]{:S(2)}, u32[]{:S(2)}) %collective-permute-start.8) | collective-permute-done | bytes 524320 | tf_op jit(solution)/shard_map/ppermute | solution.py:742
  95.4 5.4 %collective-permute-start.12 = (bf16[128,2048]{1,0:T(8,128)(2,1)S(1)}, bf16[128,2048]{1,0:T(8,128)(2,1)}, u32[]{:S(2)}, u32[]{:S(2)}) collective-permute-start(bf16[128,2048]{1,0:T(8,128)(2,1)S(1)} %multiply_convert_fusion.refs_1_.refs_5_.refs_7_.refs_6_), channel_id=1, source_target_pairs={{0,4},{4,0},{8,12},{12,8},{1,5},{5,1},{9,13},{13,9},{2,6},{6,2},{1... | collective-permute-start | bytes 1572872 | tf_op jit(solution)/shard_map/ppermute | solution.py:742
  100.9 6.2 %collective-permute-done.10.refs_3_.refs_7_.refs_9_.refs_8_ = bf16[128,2048]{1,0:T(8,128)(2,1)S(1)} collective-permute-done((bf16[128,2048]{1,0:T(8,128)(2,1)S(1)}, bf16[128,2048]{1,0:T(8,128)(2,1)S(1)}, u32[]{:S(2)}, u32[]{:S(2)}) %collective-permute-start.10) | collective-permute-done | bytes 524320 | tf_op jit(solution)/shard_map/ppermute | solution.py:742
  112.7 14.7 %ffn_front.2 = (bf16[512,2048]{1,0:T(8,128)(2,1)}, bf16[512,2048]{1,0:T(8,128)(2,1)}, bf16[512,2048]{1,0:T(8,128)(2,1)}, f32[8,128]{1,0:T(8,128)}, f32[1,1]{1,0:T(1,128)}) custom-call(f32[8,128]{1,0:T(8,128)} %get-tuple-element.99.refs_0_, bf16[128,2048]{1,0:T(8,128)(2,1)} %copy-done.10, ...), custom_call_target="tpu_custom_call" | custom-call | flops 5800000000 | bytes 1 | tf_op jit(solution)/shard_map/ffn_front/pallas_call | solution.py:96
  134.0 14.8 %ffn_front.3 = (bf16[512,2048]{1,0:T(8,128)(2,1)}, bf16[512,2048]{1,0:T(8,128)(2,1)}, bf16[512,2048]{1,0:T(8,128)(2,1)}, f32[8,128]{1,0:T(8,128)}, f32[1,1]{1,0:T(1,128)}) custom-call(f32[8,128]{1,0:T(8,128)} %get-tuple-element.100.refs_0_, bf16[128,2048]{1,0:T(8,128)(2,1)} %collective-permute-done.12.refs_1_.refs_9_.refs_11_.refs_10_, ...), custom_call_target="tpu_custom_call" | custom-call | flops 5800000000 | bytes 1 | tf_op jit(solution)/shard_map/ffn_front/pallas_call | solution.py:96
  148.8 7.0 %weight_terms.8 = (bf16[512,2048]{1,0:T(8,128)(2,1)}, f32[8,128]{1,0:T(8,128)}) custom-call(s32[2]{0:T(128)} %add_add_fusion.5.refs_0_.refs_1_, s32[2]{0:T(128)} %add_add_fusion.5.refs_0_.refs_1_, s32[4]{0:T(128)} %iota_xor_fusion.1.refs_2_.refs_0_.refs_3_.refs_1_, f32[8,128]{1,0:T(8,128)} %get-tuple-element.102.refs_3_, ...), custom_call_target="tpu_custom_call" | custom-call | flops 5800000000 | bytes 1 | tf_op jit(solution)/shard_map/weight_terms/pallas_call | solution.py:96
  157.2 11.0 %ffn_back.2 = (bf16[512,2048]{1,0:T(8,128)(2,1)}, bf16[512,2048]{1,0:T(8,128)(2,1)}, f32[8,128]{1,0:T(8,128)}) custom-call(s32[4]{0:T(128)} %iota_xor_fusion.1.refs_2_.refs_0_.refs_3_.refs_1_, f32[8,128]{1,0:T(8,128)} %get-tuple-element.105.refs_1_, ...), custom_call_target="tpu_custom_call" | custom-call | flops 5800000000 | bytes 1 | tf_op jit(solution)/shard_map/ffn_back/pallas_call | solution.py:96
  168.2 15.0 %pull.4 = (bf16[128,2048]{1,0:T(8,128)(2,1)}, bf16[128,2048]{1,0:T(8,128)(2,1)}, bf16[128,2048]{1,0:T(8,128)(2,1)}, bf16[128,2048]{1,0:T(8,128)(2,1)}, f32[8,128]{1,0:T(8,128)}, /*index=5*/f32[1,1]{1,0:T(1,128)}) custom-call(f32[8,128]{1,0:T(8,128)} %get-tuple-element.108.refs_0_, bf16[512,2048]{1,0:T(8,128)(2,1)} %get-tuple-element.109.refs_1_.refs_13_.refs_15_, ...), custom_call_target="tpu_custom_call" | custom-call | flops 5800000000 | bytes 1 | tf_op jit(solution)/shard_map/pull/pallas_call | solution.py:96
  183.7 11.0 %ffn_back.3 = (bf16[512,2048]{1,0:T(8,128)(2,1)}, bf16[512,2048]{1,0:T(8,128)(2,1)}, f32[8,128]{1,0:T(8,128)}) custom-call(s32[4]{0:T(128)} %iota_xor_fusion.1.refs_2_.refs_0_.refs_3_.refs_1_, f32[8,128]{1,0:T(8,128)} %get-tuple-element.116.refs_1_, ...), custom_call_target="tpu_custom_call" | custom-call | flops 5800000000 | bytes 1 | tf_op jit(solution)/shard_map/ffn_back/pallas_call | solution.py:96
  198.2 7.0 %weight_terms.9 = (bf16[512,2048]{1,0:T(8,128)(2,1)}, f32[8,128]{1,0:T(8,128)}) custom-call(s32[2]{0:T(128)} %add_add_fusion.5.refs_0_.refs_1_, s32[2]{0:T(128)} %add_add_fusion.5.refs_0_.refs_1_, s32[4]{0:T(128)} %iota_xor_fusion.1.refs_2_.refs_0_.refs_3_.refs_1_, bf16[128,2048]{1,0:T(8,128)(2,1)} %add_convert_fusion.2.refs_3_, ...), custom_call_target="tpu_custom_call" | custom-call | flops 5800000000 | bytes 1 | tf_op jit(solution)/shard_map/weight_terms/pallas_call | solution.py:96
  205.8 7.9 %weight_terms.10 = (bf16[256,2048]{1,0:T(8,128)(2,1)}, bf16[256,2048]{1,0:T(8,128)(2,1)}, f32[8,128]{1,0:T(8,128)}, f32[1,1]{1,0:T(1,128)}) custom-call(s32[2]{0:T(128)} %and_select_fusion.1.refs_0_, s32[2]{0:T(128)} %gather_fusion, s32[2]{0:T(128)} %gather_fusion, s32[4]{0:T(128)} %iota_xor_fusion.1.refs_2_.refs_0_.refs_3_.refs_1_, ...), custom_call_target="tpu_custom_call" | custom-call | flops 5800000000 | bytes 1 | tf_op jit(solution)/shard_map/weight_terms/pallas_call | solution.py:96
  220.5 9.5 %collective-permute-start.29 = (bf16[256,2048]{1,0:T(8,128)(2,1)}, bf16[256,2048]{1,0:T(8,128)(2,1)}, u32[]{:S(2)}, u32[]{:S(2)}) collective-permute-start(bf16[256,2048]{1,0:T(8,128)(2,1)} %get-tuple-element.132), channel_id=1, source_target_pairs={{0,8},{4,12},{8,0},{12,4},{1,9},{5,13},{9,1},{13,5},{2,10},{6,14},... | collective-permute-start | bytes 3145736 | tf_op jit(solution)/shard_map/ppermute | solution.py:742
  229.9 7.0 %weight_terms.11 = (bf16[512,2048]{1,0:T(8,128)(2,1)}, f32[8,128]{1,0:T(8,128)}) custom-call(s32[2]{0:T(128)} %add_add_fusion.5.refs_0_.refs_1_, s32[2]{0:T(128)} %add_add_fusion.5.refs_0_.refs_1_, s32[4]{0:T(128)} %iota_xor_fusion.1.refs_2_.refs_0_.refs_3_.refs_1_, bf16[128,2048]{1,0:T(8,128)(2,1)} %get-tuple-element.208.refs_3_.refs_8_.refs_5_, ...), custom_call_target="tpu_custom_call" | custom-call | flops 5800000000 | bytes 1 | tf_op jit(solution)/shard_map/weight_terms/pallas_call | solution.py:96
  240.9 15.7 %attend_back.1 = (bf16[512,512]{1,0:T(8,128)(2,1)}, f32[512,256]{1,0:T(8,128)}, bf16[512,256]{1,0:T(8,128)(2,1)}, bf16[256,256]{1,0:T(8,128)(2,1)}, bf16[256,256]{1,0:T(8,128)(2,1)}, /*index=5*/f32[8,128]{1,0:T(8,128)}) custom-call(f32[8,128]{1,0:T(8,128)} %get-tuple-element.126.refs_0_, s32[16]{0:T(128)} %concatenate.33.refs_4_.refs_1_, ...), custom_call_target="tpu_custom_call" | custom-call | flops 5800000000 | bytes 1 | tf_op jit(solution)/shard_map/attend_back/pallas_call | solution.py:96
  256.7 17.6 %collective-permute-start.26 = (bf16[256,256]{1,0:T(8,128)(2,1)}, bf16[256,256]{1,0:T(8,128)(2,1)S(1)}, u32[]{:S(2)}, u32[]{:S(2)}) collective-permute-start(bf16[256,256]{1,0:T(8,128)(2,1)} %get-tuple-element.129), channel_id=1, source_target_pairs={{0,8},{8,0},{12,4},{1,9},{9,1},{13,5},{2,10},{10,2},{14,6},{3,11},... | collective-permute-start | bytes 393224 | tf_op jit(solution)/shard_map/ppermute | solution.py:988
  279.5 8.2 %weight_terms.12 = (bf16[256,2048]{1,0:T(8,128)(2,1)}, bf16[256,2048]{1,0:T(8,128)(2,1)}, f32[8,128]{1,0:T(8,128)}, f32[1,1]{1,0:T(1,128)}) custom-call(s32[2]{0:T(128)} %and_select_fusion.1.refs_0_, s32[2]{0:T(128)} %gather_fusion, s32[2]{0:T(128)} %gather_fusion, s32[4]{0:T(128)} %iota_xor_fusion.1.refs_2_.refs_0_.refs_3_.refs_1_, ...), custom_call_target="tpu_custom_call" | custom-call | flops 5800000000 | bytes 1 | tf_op jit(solution)/shard_map/weight_terms/pallas_call | solution.py:96
  297.8 8.1 %weight_terms.13 = (bf16[256,2048]{1,0:T(8,128)(2,1)}, bf16[256,2048]{1,0:T(8,128)(2,1)}, f32[8,128]{1,0:T(8,128)}, f32[1,1]{1,0:T(1,128)}) custom-call(s32[2]{0:T(128)} %and_select_fusion.1.refs_0_, s32[2]{0:T(128)} %gather_fusion, s32[2]{0:T(128)} %gather_fusion, s32[4]{0:T(128)} %iota_xor_fusion.1.refs_2_.refs_0_.refs_3_.refs_1_, ...), custom_call_target="tpu_custom_call" | custom-call | flops 5800000000 | bytes 1 | tf_op jit(solution)/shard_map/weight_terms/pallas_call | solution.py:96
  312.6 9.6 %collective-permute-start.40 = (bf16[256,2048]{1,0:T(8,128)(2,1)}, bf16[256,2048]{1,0:T(8,128)(2,1)}, u32[]{:S(2)}, u32[]{:S(2)}) collective-permute-start(bf16[256,2048]{1,0:T(8,128)(2,1)} %get-tuple-element.158), channel_id=1, source_target_pairs={{0,8},{4,12},{8,0},{12,4},{1,9},{5,13},{9,1},{13,5},{2,10},{6,14},... | collective-permute-start | bytes 3145736 | tf_op jit(solution)/shard_map/ppermute | solution.py:742
  327.3 9.3 %push.1 = (bf16[512,2048]{1,0:T(8,128)(2,1)}, f32[8,128]{1,0:T(8,128)}) custom-call(s32[4]{0:T(128)} %iota_xor_fusion.1.refs_2_.refs_0_.refs_3_.refs_1_, f32[8,128]{1,0:T(8,128)} %get-tuple-element.142.refs_1_, bf16[512,2048]{1,0:T(8,128)(2,1)} %get-tuple-element.103.refs_12_.refs_14_.refs_2_, bf16[2048,2048]{1,0:T(8,128)(2,1)} %refs_3_.3), custom_call_target="tpu_custom_call" | custom-call | flops 5800000000 | bytes 1 | tf_op jit(solution)/shard_map/push/pallas_call | solution.py:96
  351.5 10.4 %collective-permute-done.35.refs_4_.refs_17_ = bf16[512,768]{1,0:T(8,128)(2,1)} collective-permute-done((bf16[512,768]{1,0:T(8,128)(2,1)}, bf16[512,768]{1,0:T(8,128)(2,1)}, u32[]{:S(2)}, u32[]{:S(2)}) %collective-permute-start.35) | collective-permute-done | bytes 786464 | tf_op jit(solution)/shard_map/ppermute | solution.py:742
  367.0 5.6 %collective-permute-start.44 = (bf16[256,768]{1,0:T(8,128)(2,1)}, bf16[256,768]{1,0:T(8,128)(2,1)S(1)}, u32[]{:S(2)}, u32[]{:S(2)}) collective-permute-start(bf16[256,768]{1,0:T(8,128)(2,1)} %get-tuple-element.163), channel_id=1, source_target_pairs={{0,8},{4,12},{8,0},{12,4},{1,9},{5,13},{9,1},{13,5},{2,10},{6,14},... | collective-permute-start | bytes 1179656 | tf_op jit(solution)/shard_map/ppermute | solution.py:742
  (217 shorter events, 176.4 us)
Async XLA Ops:
  7.2 141.6 %all-gather.2.cloned.1.call-start = ((), (), s32[]{:S(2)}) async-start(), calls=%async_computation.1 | async-start | bytes 6553600 | tf_op jit(solution)/shard_map/all_gather | solution.py:941
  11.4 20.9 %collective-permute-start.16 = (bf16[128,3072]{1,0:T(8,128)(2,1)}, bf16[128,3072]{1,0:T(8,128)(2,1)}, u32[]{:S(2)}, u32[]{:S(2)}) collective-permute-start(bf16[128,3072]{1,0:T(8,128)(2,1)} %pad_maximum_fusion.1), channel_id=1, source_target_pairs={{0,4},{4,0},{8,12},{12,8},{1,5},{5,1},{9,13},{13,9},{2,6},{6,2},{1... | collective-permute-start | bytes 2359304 | tf_op jit(solution)/shard_map/ppermute | solution.py:742
  15.9 22.3 %collective-permute-start = (bf16[128,2048]{1,0:T(8,128)(2,1)S(1)}, bf16[128,2048]{1,0:T(8,128)(2,1)S(1)}, u32[]{:S(2)}, u32[]{:S(2)}) collective-permute-start(bf16[128,2048]{1,0:T(8,128)(2,1)S(1)} %fusion.2.refs_0_.refs_5_.refs_7_), channel_id=1, source_target_pairs={{0,1},{1,0},{2,3},{3,2},{4,5},{5,4},{6,7},{7,6},{8,9},{9,8},{10,11... | collective-permute-start | bytes 1572872 | tf_op jit(solution)/shard_map/ppermute | solution.py:742
  34.6 389.0 %reduce-scatter.2.cloned.1.call-start = ((), (), s32[]{:S(2)}) async-start(), calls=%async_computation.2 | async-start | bytes 2621440 | tf_op jit(solution)/shard_map/reduce_scatter | solution.py:1001
  95.4 16.6 %collective-permute-start.12 = (bf16[128,2048]{1,0:T(8,128)(2,1)S(1)}, bf16[128,2048]{1,0:T(8,128)(2,1)}, u32[]{:S(2)}, u32[]{:S(2)}) collective-permute-start(bf16[128,2048]{1,0:T(8,128)(2,1)S(1)} %multiply_convert_fusion.refs_1_.refs_5_.refs_7_.refs_6_), channel_id=1, source_target_pairs={{0,4},{4,0},{8,12},{12,8},{1,5},{5,1},{9,13},{13,9},{2,6},{6,2},{1... | collective-permute-start | bytes 1572872 | tf_op jit(solution)/shard_map/ppermute | solution.py:742
  112.7 20.4 %collective-permute-start.13 = (bf16[128,2048]{1,0:T(8,128)(2,1)}, bf16[128,2048]{1,0:T(8,128)(2,1)}, u32[]{:S(2)}, u32[]{:S(2)}) collective-permute-start(bf16[128,2048]{1,0:T(8,128)(2,1)} %collective-permute-done.12.refs_1_.refs_9_.refs_11_.refs_10_), channel_id=1, source_target_pairs={{0,1},{1,0},{2,3},{3,2},{4,5},{5,4},{6,7},{7,6},{8,9},{9,8},{10,11... | collective-permute-start | bytes 1572872 | tf_op jit(solution)/shard_map/ppermute | solution.py:742
  155.7 50.0 %collective-permute-start.20 = (bf16[512,2048]{1,0:T(8,128)(2,1)}, bf16[512,2048]{1,0:T(8,128)(2,1)}, u32[]{:S(2)}, u32[]{:S(2)}) collective-permute-start(bf16[512,2048]{1,0:T(8,128)(2,1)} %get-tuple-element.115), channel_id=1, source_target_pairs={{0,16},{16,0},{1,17},{17,1},{2,18},{18,2},{3,19},{19,3},{4,20},{20... | collective-permute-start | bytes 6291464 | tf_op jit(solution)/shard_map/ppermute | solution.py:742
  183.2 30.5 %collective-permute-start.17 = (bf16[128,2048]{1,0:T(8,128)(2,1)}, bf16[128,2048]{1,0:T(8,128)(2,1)}, u32[]{:S(2)}, u32[]{:S(2)}) collective-permute-start(bf16[128,2048]{1,0:T(8,128)(2,1)} %get-tuple-element.112), channel_id=1, source_target_pairs={{0,1},{1,0},{2,3},{3,2},{4,5},{5,4},{6,7},{7,6},{8,9},{9,8},{10,11... | collective-permute-start | bytes 1572872 | tf_op jit(solution)/shard_map/ppermute | solution.py:742
  196.8 16.9 %collective-permute-start.19 = (bf16[128,2048]{1,0:T(8,128)(2,1)}, bf16[128,2048]{1,0:T(8,128)(2,1)}, u32[]{:S(2)}, u32[]{:S(2)}) collective-permute-start(bf16[128,2048]{1,0:T(8,128)(2,1)} %add_convert_fusion.2.refs_3_), channel_id=1, source_target_pairs={{0,2},{1,3},{2,0},{3,1},{4,6},{5,7},{6,4},{7,5},{8,10},{9,11},{10,... | collective-permute-start | bytes 1572872 | tf_op jit(solution)/shard_map/ppermute | solution.py:742
  205.2 70.4 %collective-permute-start.28 = (bf16[512,2048]{1,0:T(8,128)(2,1)}, bf16[512,2048]{1,0:T(8,128)(2,1)}, u32[]{:S(2)}, u32[]{:S(2)}) collective-permute-start(bf16[512,2048]{1,0:T(8,128)(2,1)} %get-tuple-element.131), channel_id=1, source_target_pairs={{0,16},{16,0},{1,17},{17,1},{2,18},{18,2},{3,19},{19,3},{4,20},{20... | collective-permute-start | bytes 6291464 | tf_op jit(solution)/shard_map/ppermute | solution.py:742
  219.9 18.6 %collective-permute-start.23 = (bf16[128,2048]{1,0:T(8,128)(2,1)}, bf16[128,2048]{1,0:T(8,128)(2,1)}, u32[]{:S(2)}, u32[]{:S(2)}) collective-permute-start(bf16[128,2048]{1,0:T(8,128)(2,1)} %get-tuple-element.208.refs_3_.refs_8_.refs_5_), channel_id=1, source_target_pairs={{0,2},{1,3},{2,0},{3,1},{4,6},{5,7},{6,4},{7,5},{8,10},{9,11},{10,... | collective-permute-start | bytes 1572872 | tf_op jit(solution)/shard_map/ppermute | solution.py:742
  220.5 20.4 %collective-permute-start.22 = (bf16[128,2048]{1,0:T(8,128)(2,1)}, bf16[128,2048]{1,0:T(8,128)(2,1)}, u32[]{:S(2)}, u32[]{:S(2)}) collective-permute-start(bf16[128,2048]{1,0:T(8,128)(2,1)} %get-tuple-element.208.refs_3_.refs_8_.refs_5_), channel_id=1, source_target_pairs={{0,1},{1,0},{2,3},{3,2},{4,5},{5,4},{6,7},{7,6},{8,9},{9,8},{10,11... | collective-permute-start | bytes 1572872 | tf_op jit(solution)/shard_map/ppermute | solution.py:742
  220.5 59.0 %collective-permute-start.29 = (bf16[256,2048]{1,0:T(8,128)(2,1)}, bf16[256,2048]{1,0:T(8,128)(2,1)}, u32[]{:S(2)}, u32[]{:S(2)}) collective-permute-start(bf16[256,2048]{1,0:T(8,128)(2,1)} %get-tuple-element.132), channel_id=1, source_target_pairs={{0,8},{4,12},{8,0},{12,4},{1,9},{5,13},{9,1},{13,5},{2,10},{6,14},... | collective-permute-start | bytes 3145736 | tf_op jit(solution)/shard_map/ppermute | solution.py:742
  237.0 60.9 %collective-permute-start.21 = (bf16[512,2048]{1,0:T(8,128)(2,1)}, bf16[512,2048]{1,0:T(8,128)(2,1)}, u32[]{:S(2)}, u32[]{:S(2)}) collective-permute-start(bf16[512,2048]{1,0:T(8,128)(2,1)} %get-tuple-element.125), channel_id=1, source_target_pairs={{0,16},{16,0},{1,17},{17,1},{2,18},{18,2},{3,19},{19,3},{4,20},{20... | collective-permute-start | bytes 6291464 | tf_op jit(solution)/shard_map/ppermute | solution.py:742
  256.7 31.2 %collective-permute-start.26 = (bf16[256,256]{1,0:T(8,128)(2,1)}, bf16[256,256]{1,0:T(8,128)(2,1)S(1)}, u32[]{:S(2)}, u32[]{:S(2)}) collective-permute-start(bf16[256,256]{1,0:T(8,128)(2,1)} %get-tuple-element.129), channel_id=1, source_target_pairs={{0,8},{8,0},{12,4},{1,9},{9,1},{13,5},{2,10},{10,2},{14,6},{3,11},... | collective-permute-start | bytes 393224 | tf_op jit(solution)/shard_map/ppermute | solution.py:988
  287.7 63.2 %collective-permute-start.36 = (bf16[256,2048]{1,0:T(8,128)(2,1)}, bf16[256,2048]{1,0:T(8,128)(2,1)}, u32[]{:S(2)}, u32[]{:S(2)}) collective-permute-start(bf16[256,2048]{1,0:T(8,128)(2,1)} %get-tuple-element.153), channel_id=1, source_target_pairs={{0,8},{4,12},{8,0},{12,4},{1,9},{5,13},{9,1},{13,5},{2,10},{6,14},... | collective-permute-start | bytes 3145736 | tf_op jit(solution)/shard_map/ppermute | solution.py:742
  294.2 42.5 %collective-permute-start.33 = (bf16[512,768]{1,0:T(8,128)(2,1)}, bf16[512,768]{1,0:T(8,128)(2,1)}, u32[]{:S(2)}, u32[]{:S(2)}) collective-permute-start(bf16[512,768]{1,0:T(8,128)(2,1)} %get-tuple-element.148.refs_13_.refs_15_), channel_id=1, source_target_pairs={{0,4},{4,0},{8,12},{12,8},{1,5},{5,1},{9,13},{13,9},{2,6},{6,2},{1... | collective-permute-start | bytes 2359304 | tf_op jit(solution)/shard_map/ppermute | solution.py:742
  310.8 66.6 %collective-permute-start.34 = (bf16[1024,512]{1,0:T(8,128)(2,1)}, bf16[1024,512]{1,0:T(8,128)(2,1)}, u32[]{:S(2)}, u32[]{:S(2)}) collective-permute-start(bf16[1024,512]{1,0:T(8,128)(2,1)} %get-tuple-element.151), channel_id=1, source_target_pairs={{0,4},{4,0},{8,12},{12,8},{1,5},{5,1},{9,13},{13,9},{2,6},{6,2},{1... | collective-permute-start | bytes 3145736 | tf_op jit(solution)/shard_map/ppermute | solution.py:742
  312.6 81.1 %collective-permute-start.40 = (bf16[256,2048]{1,0:T(8,128)(2,1)}, bf16[256,2048]{1,0:T(8,128)(2,1)}, u32[]{:S(2)}, u32[]{:S(2)}) collective-permute-start(bf16[256,2048]{1,0:T(8,128)(2,1)} %get-tuple-element.158), channel_id=1, source_target_pairs={{0,8},{4,12},{8,0},{12,4},{1,9},{5,13},{9,1},{13,5},{2,10},{6,14},... | collective-permute-start | bytes 3145736 | tf_op jit(solution)/shard_map/ppermute | solution.py:742
  341.7 20.2 %collective-permute-start.35 = (bf16[512,768]{1,0:T(8,128)(2,1)}, bf16[512,768]{1,0:T(8,128)(2,1)}, u32[]{:S(2)}, u32[]{:S(2)}) collective-permute-start(bf16[512,768]{1,0:T(8,128)(2,1)} %get-tuple-element.152), channel_id=1, source_target_pairs={{0,16},{16,0},{1,17},{17,1},{2,18},{18,2},{3,19},{19,3},{4,20},{20... | collective-permute-start | bytes 2359304 | tf_op jit(solution)/shard_map/ppermute | solution.py:742
  348.7 23.8 %collective-permute-start.30 = (bf16[128,2048]{1,0:T(8,128)(2,1)}, bf16[128,2048]{1,0:T(8,128)(2,1)}, u32[]{:S(2)}, u32[]{:S(2)}) collective-permute-start(bf16[128,2048]{1,0:T(8,128)(2,1)} %get-tuple-element.145), channel_id=1, source_target_pairs={{0,1},{1,0},{2,3},{3,2},{4,5},{5,4},{6,7},{7,6},{8,9},{9,8},{10,11... | collective-permute-start | bytes 1572872 | tf_op jit(solution)/shard_map/ppermute | solution.py:742
  351.0 23.8 %collective-permute-start.32 = (bf16[128,2048]{1,0:T(8,128)(2,1)}, bf16[128,2048]{1,0:T(8,128)(2,1)}, u32[]{:S(2)}, u32[]{:S(2)}) collective-permute-start(bf16[128,2048]{1,0:T(8,128)(2,1)} %add_convert_fusion), channel_id=1, source_target_pairs={{0,2},{1,3},{2,0},{3,1},{4,6},{5,7},{6,4},{7,5},{8,10},{9,11},{10,... | collective-permute-start | bytes 1572872 | tf_op jit(solution)/shard_map/ppermute | solution.py:742
  367.0 47.9 %collective-permute-start.44 = (bf16[256,768]{1,0:T(8,128)(2,1)}, bf16[256,768]{1,0:T(8,128)(2,1)S(1)}, u32[]{:S(2)}, u32[]{:S(2)}) collective-permute-start(bf16[256,768]{1,0:T(8,128)(2,1)} %get-tuple-element.163), channel_id=1, source_target_pairs={{0,8},{4,12},{8,0},{12,4},{1,9},{5,13},{9,1},{13,5},{2,10},{6,14},... | collective-permute-start | bytes 1179656 | tf_op jit(solution)/shard_map/ppermute | solution.py:742
  403.5 18.4 %collective-permute-start.45 = (bf16[256,512]{1,0:T(8,128)(2,1)}, bf16[256,512]{1,0:T(8,128)(2,1)S(1)}, u32[]{:S(2)}, u32[]{:S(2)}) collective-permute-start(bf16[256,512]{1,0:T(8,128)(2,1)} %get-tuple-element.165), channel_id=1, source_target_pairs={{0,8},{4,12},{8,0},{12,4},{1,9},{5,13},{9,1},{13,5},{2,10},{6,14},... | collective-permute-start | bytes 786440 | tf_op jit(solution)/shard_map/ppermute | solution.py:742
  (54 other events, 439.2 us)
Sparse Core Ops, SparseCore 0:
  34.7 42.3 all-gather.1
  336.8 37.1 reduce-scatter.1
where the time goes:
time: 438 us; the launch traced here: 433 us
  Pallas kernels  187 us (43%)
  starting transfers between devices  92.2 us (21%)
  waiting for transfers between devices  71.1 us (16%)
  other arithmetic  50.3 us (11%)
  between operations  16.7 us (4%)
  local copies, waits for them, and re-layouts  14.8 us (3%)
    pallas_call x23, Pallas kernels, call(): pl.pallas_call(inner, grid_spec=pltpu.PrefetchScalarGridSpec(num_scalar_p...  187 us
    ppermute x40, waiting for transfers between devices, flip(): return lax.ppermute(values_in, axis, [(i, i ^ mask) for i in range(count)])  64.4 us
    ppermute x40, starting transfers between devices, flip(): return lax.ppermute(values_in, axis, [(i, i ^ mask) for i in range(count)])  61.7 us
    ppermute x3, starting transfers between devices, per_device(): lax.ppermute(part, 'ctx', [(target, source) for source, target in moves])  21.6 us
    ppermute x3, starting transfers between devices, per_device(): tiles.append(lax.ppermute(held, 'ctx', moves))  8.81 us
  transfers between devices with their start and end apart: 48, of which 17 were waited for; matrix products, arithmetic and copies ran while one was open for 13% of the time, Pallas kernels for 42%

commit v1 on v0

--- a/solution.py
+++ b/solution.py
@@ -73,6 +73,7 @@
     def __init__(self):
         self.held = []
         self.cost = 58 * 10**8
+        self.room = VMEM_BYTES // 2
 
     def wait(self, *arrays):
         self.held = [*arrays, *self.held]
@@ -104,7 +105,7 @@
             ),
             out_shape=[*out_shape, *marks],
             compiler_params=pltpu.CompilerParams(
-                vmem_limit_bytes=VMEM_BYTES, dimension_semantics=("arbitrary",) * len(grid)
+                vmem_limit_bytes=self.room, dimension_semantics=("arbitrary",) * len(grid)
             ),
             cost_estimate=pl.CostEstimate(flops=self.cost, bytes_accessed=1, transcendentals=0),
             name=name,
@@ -960,6 +961,7 @@
 
     normed_ffn_local = rms_norm(hidden_state, ffn_gain).astype(BF16)
     normed_ffn = tp_gather(normed_ffn_local)
+    chain.room = 52 * 1024 * 1024
     act, slope, silu = ffn_front(chain, normed_ffn, w_gate, w_up)
     normed_ffn_pair = tp_gather(flip(normed_ffn_local, "ctx", 1), chain.zero)
     act_pair, slope_pair, silu_pair = ffn_front(chain, normed_ffn_pair, w_gate, w_up)
@@ -984,6 +986,7 @@
     grad_query, own, *sent = attend_back(
         chain, places, docs, halves, query, merged, totals, cos, sin, w_out, grad_sb, kv, tiles
     )
+    chain.room = VMEM_BYTES * 3 // 4
     returned = [
         lax.ppermute(part, "ctx", [(target, source) for source, target in moves])
         for part, (moves, _) in zip(sent, plan)

time: 438 us -> 417 us (0.952)
  Pallas kernels: 187 us -> 166 us
  other arithmetic: 50.3 us -> 33.9 us
  local copies, waits for them, and re-layouts: 14.8 us -> 28.7 us
  waiting for transfers between devices: 71.1 us -> 84 us
  starting transfers between devices: 92.2 us -> 81.3 us
    pallas_call x23, Pallas kernels: 187 us -> 166 us  [call(): pl.pallas_call(inner, grid_spec=pltpu.PrefetchScalarGridSpec(num_scalar_p...]
    unnamed x62 -> x146, local copies, waits for them, and re-layouts: 8.39 us -> 23.8 us
    ppermute x40, waiting for transfers between devices: 64.4 us -> 76.6 us  [flip(): return lax.ppermute(values_in, axis, [(i, i ^ mask) for i in range(count)])]
    ppermute x40, starting transfers between devices: 61.7 us -> 52 us  [flip(): return lax.ppermute(values_in, axis, [(i, i ^ mask) for i in range(count)])]
  transfers between devices with their start and end apart: 48 -> 48, of which waited for: 17 -> 20; matrix products, arithmetic and copies ran while one was open for 13% -> 9% of each run, Pallas kernels for 42% -> 39%
where the time goes in v1:
time: 417 us; the launch traced here: 411 us
  Pallas kernels  166 us (40%)
  waiting for transfers between devices  84 us (20%)
  starting transfers between devices  81.3 us (19%)
  other arithmetic  33.9 us (8%)
  local copies, waits for them, and re-layouts  28.7 us (7%)
  between operations  17.2 us (4%)
    pallas_call x23, Pallas kernels, call(): pl.pallas_call(inner, grid_spec=pltpu.PrefetchScalarGridSpec(num_scalar_p...  166 us
    ppermute x40, waiting for transfers between devices, flip(): return lax.ppermute(values_in, axis, [(i, i ^ mask) for i in range(count)])  76.6 us
    ppermute x40, starting transfers between devices, flip(): return lax.ppermute(values_in, axis, [(i, i ^ mask) for i in range(count)])  52 us
    unnamed x146, local copies, waits for them, and re-layouts  23.8 us
    ppermute x3, starting transfers between devices, per_device(): lax.ppermute(part, 'ctx', [(target, source) for source, target in moves])  20.4 us
    ppermute x3, starting transfers between devices, per_device(): tiles.append(lax.ppermute(held, 'ctx', moves))  8.82 us
  transfers between devices with their start and end apart: 48, of which 20 were waited for; matrix products, arithmetic and copies ran while one was open for 9% of the time, Pallas kernels for 39%

profile of v1, /device:TPU:0, one launch (start us, length us, event | category | flops | bytes accessed | tf_op | source)
XLA Modules:
  0.0 411.4 jit_solution(5305320269905215205)
XLA Ops:
  18.3 10.0 %collective-permute-done.1.refs_2_.refs_7_.refs_9_ = bf16[128,2048]{1,0:T(8,128)(2,1)S(1)} collective-permute-done((bf16[128,2048]{1,0:T(8,128)(2,1)S(1)}, bf16[128,2048]{1,0:T(8,128)(2,1)S(1)}, u32[]{:S(2)}, u32[]{:S(2)}) %collective-permute-start.1) | collective-permute-done | bytes 524320 | tf_op jit(solution)/shard_map/ppermute | solution.py:743
  60.5 7.3 %attend.1 = (bf16[512,512]{1,0:T(8,128)(2,1)S(1)}, f32[4,1,1024]{2,1,0:T(1,128)S(1)}, f32[8,128]{1,0:T(8,128)S(1)}) custom-call(bf16[512,256]{1,0:T(8,128)(2,1)S(1)} %collective-permute-done.3.refs_0_.refs_7_.refs_13_, bf16[256,256]{1,0:T(8,128)(2,1)S(1)} %collective-permute-done.4.refs_1_.refs_8_.refs_14_, ...), custom_call_target="tpu_custom_call" | custom-call | flops 5800000000 | bytes 1 | tf_op jit(solution)/shard_map/attend/pallas_call | solution.py:97
  73.8 12.9 %collective-permute-done.8 = bf16[128,2048]{1,0:T(8,128)(2,1)S(1)} collective-permute-done((bf16[128,2048]{1,0:T(8,128)(2,1)S(1)}, bf16[128,2048]{1,0:T(8,128)(2,1)S(1)}, u32[]{:S(2)}, u32[]{:S(2)}) %collective-permute-start.8) | collective-permute-done | bytes 524320 | tf_op jit(solution)/shard_map/ppermute | solution.py:743
  88.5 5.4 %collective-permute-start.12 = (bf16[128,2048]{1,0:T(8,128)(2,1)S(1)}, bf16[128,2048]{1,0:T(8,128)(2,1)}, u32[]{:S(2)}, u32[]{:S(2)}) collective-permute-start(bf16[128,2048]{1,0:T(8,128)(2,1)S(1)} %multiply_convert_fusion.refs_1_.refs_5_.refs_7_.refs_6_), channel_id=1, source_target_pairs={{0,4},{4,0},{8,12},{12,8},{1,5},{5,1},{9,13},{13,9},{2,6},{6,2},{1... | collective-permute-start | bytes 1572872 | tf_op jit(solution)/shard_map/ppermute | solution.py:743
  94.0 7.1 %collective-permute-done.10.refs_3_.refs_7_.refs_9_.refs_8_ = bf16[128,2048]{1,0:T(8,128)(2,1)S(1)} collective-permute-done((bf16[128,2048]{1,0:T(8,128)(2,1)S(1)}, bf16[128,2048]{1,0:T(8,128)(2,1)S(1)}, u32[]{:S(2)}, u32[]{:S(2)}) %collective-permute-start.10) | collective-permute-done | bytes 524320 | tf_op jit(solution)/shard_map/ppermute | solution.py:743
  105.7 14.4 %ffn_front.2 = (bf16[512,2048]{1,0:T(8,128)(2,1)}, bf16[512,2048]{1,0:T(8,128)(2,1)}, bf16[512,2048]{1,0:T(8,128)(2,1)}, f32[8,128]{1,0:T(8,128)S(1)}, f32[1,1]{1,0:T(1,128)}) custom-call(f32[8,128]{1,0:T(8,128)S(1)} %get-tuple-element.99.refs_0_, bf16[128,2048]{1,0:T(8,128)(2,1)S(1)} %multiply_convert_fusion.refs_1_.refs_5_.refs_7_.refs_6_, ...), custom_call_target="tpu_custom_call" | custom-call | flops 5800000000 | bytes 1 | tf_op jit(solution)/shard_map/ffn_front/pallas_call | solution.py:97
  124.7 14.6 %ffn_front.3 = (bf16[512,2048]{1,0:T(8,128)(2,1)}, bf16[512,2048]{1,0:T(8,128)(2,1)}, bf16[512,2048]{1,0:T(8,128)(2,1)}, f32[8,128]{1,0:T(8,128)S(1)}, f32[1,1]{1,0:T(1,128)}) custom-call(f32[8,128]{1,0:T(8,128)S(1)} %get-tuple-element.100.refs_0_, bf16[128,2048]{1,0:T(8,128)(2,1)} %collective-permute-done.12.refs_1_.refs_9_.refs_11_.refs_10_, ...), custom_call_target="tpu_custom_call" | custom-call | flops 5800000000 | bytes 1 | tf_op jit(solution)/shard_map/ffn_front/pallas_call | solution.py:97
  139.4 6.8 %weight_terms.8 = (bf16[512,2048]{1,0:T(8,128)(2,1)}, f32[8,128]{1,0:T(8,128)S(1)}) custom-call(s32[2]{0:T(128)S(1)} %add_add_fusion.5.refs_0_.refs_1_, s32[2]{0:T(128)S(1)} %add_add_fusion.5.refs_0_.refs_1_, s32[4]{0:T(128)S(1)} %iota_xor_fusion.1.refs_2_.refs_0_.refs_3_.refs_1_, f32[8,128]{1,0:T(8,128)S(1)} %get-tuple-element.102.refs_3_, ...), custom_call_target="tpu_custom_call" | custom-call | flops 5800000000 | bytes 1 | tf_op jit(solution)/shard_map/weight_terms/pallas_call | solution.py:97
  147.7 10.9 %ffn_back.2 = (bf16[512,2048]{1,0:T(8,128)(2,1)}, bf16[512,2048]{1,0:T(8,128)(2,1)}, f32[8,128]{1,0:T(8,128)S(1)}) custom-call(s32[4]{0:T(128)S(1)} %iota_xor_fusion.1.refs_2_.refs_0_.refs_3_.refs_1_, f32[8,128]{1,0:T(8,128)S(1)} %get-tuple-element.105.refs_1_, ...), custom_call_target="tpu_custom_call" | custom-call | flops 5800000000 | bytes 1 | tf_op jit(solution)/shard_map/ffn_back/pallas_call | solution.py:97
  158.5 14.9 %pull.4 = (bf16[128,2048]{1,0:T(8,128)(2,1)S(1)}, bf16[128,2048]{1,0:T(8,128)(2,1)S(1)}, bf16[128,2048]{1,0:T(8,128)(2,1)S(1)}, bf16[128,2048]{1,0:T(8,128)(2,1)}, f32[8,128]{1,0:T(8,128)S(1)}, /*index=5*/f32[1,1]{1,0:T(1,128)}) custom-call(f32[8,128]{1,0:T(8,128)S(1)} %get-tuple-element.108.refs_0_, ...), custom_call_target="tpu_custom_call" | custom-call | flops 5800000000 | bytes 1 | tf_op jit(solution)/shard_map/pull/pallas_call | solution.py:97
  174.0 10.9 %ffn_back.3 = (bf16[512,2048]{1,0:T(8,128)(2,1)}, bf16[512,2048]{1,0:T(8,128)(2,1)}, f32[8,128]{1,0:T(8,128)S(1)}) custom-call(s32[4]{0:T(128)S(1)} %iota_xor_fusion.1.refs_2_.refs_0_.refs_3_.refs_1_, f32[8,128]{1,0:T(8,128)S(1)} %get-tuple-element.116.refs_1_, ...), custom_call_target="tpu_custom_call" | custom-call | flops 5800000000 | bytes 1 | tf_op jit(solution)/shard_map/ffn_back/pallas_call | solution.py:97
  186.7 6.8 %weight_terms.9 = (bf16[512,2048]{1,0:T(8,128)(2,1)}, f32[8,128]{1,0:T(8,128)S(1)}) custom-call(s32[2]{0:T(128)S(1)} %add_add_fusion.5.refs_0_.refs_1_, s32[2]{0:T(128)S(1)} %add_add_fusion.5.refs_0_.refs_1_, s32[4]{0:T(128)S(1)} %iota_xor_fusion.1.refs_2_.refs_0_.refs_3_.refs_1_, bf16[128,2048]{1,0:T(8,128)(2,1)S(1)} %add_convert_fusion.2.refs_3_, ...), custom_call_target="tpu_custom_call" | custom-call | flops 5800000000 | bytes 1 | tf_op jit(solution)/shard_map/weight_terms/pallas_call | solution.py:97
  195.6 7.8 %weight_terms.10 = (bf16[256,2048]{1,0:T(8,128)(2,1)}, bf16[256,2048]{1,0:T(8,128)(2,1)}, f32[8,128]{1,0:T(8,128)S(1)}, f32[1,1]{1,0:T(1,128)}) custom-call(s32[2]{0:T(128)S(1)} %and_select_fusion.1.refs_0_, s32[2]{0:T(128)S(1)} %gather_fusion, s32[2]{0:T(128)S(1)} %gather_fusion, s32[4]{0:T(128)S(1)} %iota_xor_fusion.1.refs_2_.refs_0_.refs_3_.refs_1_, ...), custom_call_target="tpu_custom_call" | custom-call | flops 5800000000 | bytes 1 | tf_op jit(solution)/shard_map/weight_terms/pallas_call | solution.py:97
  208.3 9.5 %collective-permute-start.29 = (bf16[256,2048]{1,0:T(8,128)(2,1)}, bf16[256,2048]{1,0:T(8,128)(2,1)S(1)}, u32[]{:S(2)}, u32[]{:S(2)}) collective-permute-start(bf16[256,2048]{1,0:T(8,128)(2,1)} %get-tuple-element.132), channel_id=1, source_target_pairs={{0,8},{4,12},{8,0},{12,4},{1,9},{5,13},{9,1},{13,5},{2,10},{6,14},... | collective-permute-start | bytes 3145736 | tf_op jit(solution)/shard_map/ppermute | solution.py:743
  217.9 6.8 %weight_terms.11 = (bf16[512,2048]{1,0:T(8,128)(2,1)}, f32[8,128]{1,0:T(8,128)S(1)}) custom-call(s32[2]{0:T(128)S(1)} %add_add_fusion.5.refs_0_.refs_1_, s32[2]{0:T(128)S(1)} %add_add_fusion.5.refs_0_.refs_1_, s32[4]{0:T(128)S(1)} %iota_xor_fusion.1.refs_2_.refs_0_.refs_3_.refs_1_, bf16[128,2048]{1,0:T(8,128)(2,1)S(1)} %get-tuple-element.208.refs_3_.refs_8_.refs_5_, ...), custom_call_target="tpu_custom_call" | custom-call | flops 5800000000 | bytes 1 | tf_op jit(solution)/shard_map/weight_terms/pallas_call | solution.py:97
  231.4 15.3 %attend_back.1 = (bf16[512,512]{1,0:T(8,128)(2,1)}, f32[512,256]{1,0:T(8,128)}, bf16[512,256]{1,0:T(8,128)(2,1)S(1)}, bf16[256,256]{1,0:T(8,128)(2,1)S(1)}, bf16...) custom-call(f32[8,128]{1,0:T(8,128)S(1)} %get-tuple-element.126.refs_0_, s32[16]{0:T(128)S(1)} %concatenate.33.refs_4_.refs_1_, ...), custom_call_target="tpu_custom_call" | custom-call | flops 5800000000 | bytes 1 | tf_op jit(solution)/shard_map/attend_back/pallas_call | solution.py:97
  246.7 16.5 %collective-permute-start.26 = (bf16[256,256]{1,0:T(8,128)(2,1)S(1)}, bf16[256,256]{1,0:T(8,128)(2,1)S(1)}, u32[]{:S(2)}, u32[]{:S(2)}) collective-permute-start(bf16[256,256]{1,0:T(8,128)(2,1)S(1)} %get-tuple-element.129), channel_id=1, source_target_pairs={{0,8},{8,0},{12,4},{1,9},{9,1},{13,5},{2,10},{10,2},{14,6},{3,11},... | collective-permute-start | bytes 393224 | tf_op jit(solution)/shard_map/ppermute | solution.py:991
  267.2 7.4 %weight_terms.12 = (bf16[256,2048]{1,0:T(8,128)(2,1)}, bf16[256,2048]{1,0:T(8,128)(2,1)S(1)}, f32[8,128]{1,0:T(8,128)S(1)}, f32[1,1]{1,0:T(1,128)}) custom-call(s32[2]{0:T(128)S(1)} %and_select_fusion.1.refs_0_, s32[2]{0:T(128)S(1)} %gather_fusion, s32[2]{0:T(128)S(1)} %gather_fusion, s32[4]{0:T(128)S(1)} %iota_xor_fusion.1.refs_2_.refs_0_.refs_3_.refs_1_, ...), custom_call_target="tpu_custom_call" | custom-call | flops 5800000000 | bytes 1 | tf_op jit(solution)/shard_map/weight_terms/pallas_call | solution.py:97
  280.9 5.1 %collective-permute-done.21.refs_4_.refs_16_ = bf16[512,2048]{1,0:T(8,128)(2,1)} collective-permute-done((bf16[512,2048]{1,0:T(8,128)(2,1)}, bf16[512,2048]{1,0:T(8,128)(2,1)}, u32[]{:S(2)}, u32[]{:S(2)}) %collective-permute-start.21) | collective-permute-done | bytes 2097184 | tf_op jit(solution)/shard_map/ppermute | solution.py:743
  286.1 7.2 %weight_terms.13 = (bf16[256,2048]{1,0:T(8,128)(2,1)}, bf16[256,2048]{1,0:T(8,128)(2,1)S(1)}, f32[8,128]{1,0:T(8,128)S(1)}, f32[1,1]{1,0:T(1,128)}) custom-call(s32[2]{0:T(128)S(1)} %and_select_fusion.1.refs_0_, s32[2]{0:T(128)S(1)} %gather_fusion, s32[2]{0:T(128)S(1)} %gather_fusion, s32[4]{0:T(128)S(1)} %iota_xor_fusion.1.refs_2_.refs_0_.refs_3_.refs_1_, ...), custom_call_target="tpu_custom_call" | custom-call | flops 5800000000 | bytes 1 | tf_op jit(solution)/shard_map/weight_terms/pallas_call | solution.py:97
  294.3 4.8 %own_terms.2 = (bf16[1024,512]{1,0:T(8,128)(2,1)}, f32[8,128]{1,0:T(8,128)S(1)}, f32[1,1]{1,0:T(1,128)}) custom-call(s32[4]{0:T(128)S(1)} %fusion.22.refs_0_, s32[4]{0:T(128)S(1)} %iota_xor_fusion.1.refs_2_.refs_0_.refs_3_.refs_1_, f32[8,128]{1,0:T(8,128)S(1)} %get-tuple-element.138.refs_2_, bf16[128,2048]{1,0:T(8,128)(2,1)S(1)} %copy-done.25, ...), custom_call_target="tpu_custom_call" | custom-call | flops 5800000000 | bytes 1 | tf_op jit(solution)/shard_map/own_terms/pallas_call | solution.py:97
  300.8 9.5 %collective-permute-start.40 = (bf16[256,2048]{1,0:T(8,128)(2,1)}, bf16[256,2048]{1,0:T(8,128)(2,1)}, u32[]{:S(2)}, u32[]{:S(2)}) collective-permute-start(bf16[256,2048]{1,0:T(8,128)(2,1)} %get-tuple-element.158), channel_id=1, source_target_pairs={{0,8},{4,12},{8,0},{12,4},{1,9},{5,13},{9,1},{13,5},{2,10},{6,14},... | collective-permute-start | bytes 3145736 | tf_op jit(solution)/shard_map/ppermute | solution.py:743
  313.6 7.7 %push.1 = (bf16[512,2048]{1,0:T(8,128)(2,1)S(1)}, f32[8,128]{1,0:T(8,128)S(1)}) custom-call(s32[4]{0:T(128)S(1)} %iota_xor_fusion.1.refs_2_.refs_0_.refs_3_.refs_1_, f32[8,128]{1,0:T(8,128)S(1)} %get-tuple-element.142.refs_1_, bf16[512,2048]{1,0:T(8,128)(2,1)S(1)} %copy-done, bf16[2048,2048]{1,0:T(8,128)(2,1)} %refs_3_.3), custom_call_target="tpu_custom_call" | custom-call | flops 5800000000 | bytes 1 | tf_op jit(solution)/shard_map/push/pallas_call | solution.py:97
  337.8 12.5 %collective-permute-done.35.refs_4_.refs_17_ = bf16[512,768]{1,0:T(8,128)(2,1)} collective-permute-done((bf16[512,768]{1,0:T(8,128)(2,1)}, bf16[512,768]{1,0:T(8,128)(2,1)}, u32[]{:S(2)}, u32[]{:S(2)}) %collective-permute-start.35) | collective-permute-done | bytes 786464 | tf_op jit(solution)/shard_map/ppermute | solution.py:743
  (301 shorter events, 162.1 us)
Async XLA Ops:
  7.2 132.2 %all-gather.2.cloned.1.call-start = ((), (), s32[]{:S(2)}) async-start(), calls=%async_computation.1 | async-start | bytes 6553600 | tf_op jit(solution)/shard_map/all_gather | solution.py:942
  11.9 20.9 %collective-permute-start.16 = (bf16[128,3072]{1,0:T(8,128)(2,1)}, bf16[128,3072]{1,0:T(8,128)(2,1)}, u32[]{:S(2)}, u32[]{:S(2)}) collective-permute-start(bf16[128,3072]{1,0:T(8,128)(2,1)} %pad_maximum_fusion.1), channel_id=1, source_target_pairs={{0,4},{4,0},{8,12},{12,8},{1,5},{5,1},{9,13},{13,9},{2,6},{6,2},{1... | collective-permute-start | bytes 2359304 | tf_op jit(solution)/shard_map/ppermute | solution.py:743
  16.4 22.7 %collective-permute-start = (bf16[128,2048]{1,0:T(8,128)(2,1)S(1)}, bf16[128,2048]{1,0:T(8,128)(2,1)S(1)}, u32[]{:S(2)}, u32[]{:S(2)}) collective-permute-start(bf16[128,2048]{1,0:T(8,128)(2,1)S(1)} %fusion.2.refs_0_.refs_5_.refs_7_), channel_id=1, source_target_pairs={{0,1},{1,0},{2,3},{3,2},{4,5},{5,4},{6,7},{7,6},{8,9},{9,8},{10,11... | collective-permute-start | bytes 1572872 | tf_op jit(solution)/shard_map/ppermute | solution.py:743
  35.1 367.3 %reduce-scatter.2.cloned.1.call-start = ((), (), s32[]{:S(2)}) async-start(), calls=%async_computation.2 | async-start | bytes 2621440 | tf_op jit(solution)/shard_map/reduce_scatter | solution.py:1004
  88.5 16.6 %collective-permute-start.12 = (bf16[128,2048]{1,0:T(8,128)(2,1)S(1)}, bf16[128,2048]{1,0:T(8,128)(2,1)}, u32[]{:S(2)}, u32[]{:S(2)}) collective-permute-start(bf16[128,2048]{1,0:T(8,128)(2,1)S(1)} %multiply_convert_fusion.refs_1_.refs_5_.refs_7_.refs_6_), channel_id=1, source_target_pairs={{0,4},{4,0},{8,12},{12,8},{1,5},{5,1},{9,13},{13,9},{2,6},{6,2},{1... | collective-permute-start | bytes 1572872 | tf_op jit(solution)/shard_map/ppermute | solution.py:743
  105.7 17.2 %collective-permute-start.13 = (bf16[128,2048]{1,0:T(8,128)(2,1)}, bf16[128,2048]{1,0:T(8,128)(2,1)}, u32[]{:S(2)}, u32[]{:S(2)}) collective-permute-start(bf16[128,2048]{1,0:T(8,128)(2,1)} %collective-permute-done.12.refs_1_.refs_9_.refs_11_.refs_10_), channel_id=1, source_target_pairs={{0,1},{1,0},{2,3},{3,2},{4,5},{5,4},{6,7},{7,6},{8,9},{9,8},{10,11... | collective-permute-start | bytes 1572872 | tf_op jit(solution)/shard_map/ppermute | solution.py:743
  146.2 48.1 %collective-permute-start.20 = (bf16[512,2048]{1,0:T(8,128)(2,1)}, bf16[512,2048]{1,0:T(8,128)(2,1)S(1)}, u32[]{:S(2)}, u32[]{:S(2)}) collective-permute-start(bf16[512,2048]{1,0:T(8,128)(2,1)} %get-tuple-element.115), channel_id=1, source_target_pairs={{0,16},{16,0},{1,17},{17,1},{2,18},{18,2},{3,19},{19,3},{4,20},{20... | collective-permute-start | bytes 6291464 | tf_op jit(solution)/shard_map/ppermute | solution.py:743
  173.5 29.9 %collective-permute-start.17 = (bf16[128,2048]{1,0:T(8,128)(2,1)S(1)}, bf16[128,2048]{1,0:T(8,128)(2,1)S(1)}, u32[]{:S(2)}, u32[]{:S(2)}) collective-permute-start(bf16[128,2048]{1,0:T(8,128)(2,1)S(1)} %get-tuple-element.112), channel_id=1, source_target_pairs={{0,1},{1,0},{2,3},{3,2},{4,5},{5,4},{6,7},{7,6},{8,9},{9,8},{10,11... | collective-permute-start | bytes 1572872 | tf_op jit(solution)/shard_map/ppermute | solution.py:743
  185.1 18.4 %collective-permute-start.19 = (bf16[128,2048]{1,0:T(8,128)(2,1)S(1)}, bf16[128,2048]{1,0:T(8,128)(2,1)S(1)}, u32[]{:S(2)}, u32[]{:S(2)}) collective-permute-start(bf16[128,2048]{1,0:T(8,128)(2,1)S(1)} %add_convert_fusion.2.refs_3_), channel_id=1, source_target_pairs={{0,2},{1,3},{2,0},{3,1},{4,6},{5,7},{6,4},{7,5},{8,10},{9,11},{10,... | collective-permute-start | bytes 1572872 | tf_op jit(solution)/shard_map/ppermute | solution.py:743
  193.5 71.0 %collective-permute-start.28 = (bf16[512,2048]{1,0:T(8,128)(2,1)}, bf16[512,2048]{1,0:T(8,128)(2,1)}, u32[]{:S(2)}, u32[]{:S(2)}) collective-permute-start(bf16[512,2048]{1,0:T(8,128)(2,1)} %get-tuple-element.131), channel_id=1, source_target_pairs={{0,16},{16,0},{1,17},{17,1},{2,18},{18,2},{3,19},{19,3},{4,20},{20... | collective-permute-start | bytes 6291464 | tf_op jit(solution)/shard_map/ppermute | solution.py:743
  206.8 19.6 %collective-permute-start.23 = (bf16[128,2048]{1,0:T(8,128)(2,1)S(1)}, bf16[128,2048]{1,0:T(8,128)(2,1)}, u32[]{:S(2)}, u32[]{:S(2)}) collective-permute-start(bf16[128,2048]{1,0:T(8,128)(2,1)S(1)} %get-tuple-element.208.refs_3_.refs_8_.refs_5_), channel_id=1, source_target_pairs={{0,2},{1,3},{2,0},{3,1},{4,6},{5,7},{6,4},{7,5},{8,10},{9,11},{10,... | collective-permute-start | bytes 1572872 | tf_op jit(solution)/shard_map/ppermute | solution.py:743
  208.3 18.9 %collective-permute-start.22 = (bf16[128,2048]{1,0:T(8,128)(2,1)S(1)}, bf16[128,2048]{1,0:T(8,128)(2,1)}, u32[]{:S(2)}, u32[]{:S(2)}) collective-permute-start(bf16[128,2048]{1,0:T(8,128)(2,1)S(1)} %get-tuple-element.208.refs_3_.refs_8_.refs_5_), channel_id=1, source_target_pairs={{0,1},{1,0},{2,3},{3,2},{4,5},{5,4},{6,7},{7,6},{8,9},{9,8},{10,11... | collective-permute-start | bytes 1572872 | tf_op jit(solution)/shard_map/ppermute | solution.py:743
  208.3 58.9 %collective-permute-start.29 = (bf16[256,2048]{1,0:T(8,128)(2,1)}, bf16[256,2048]{1,0:T(8,128)(2,1)S(1)}, u32[]{:S(2)}, u32[]{:S(2)}) collective-permute-start(bf16[256,2048]{1,0:T(8,128)(2,1)} %get-tuple-element.132), channel_id=1, source_target_pairs={{0,8},{4,12},{8,0},{12,4},{1,9},{5,13},{9,1},{13,5},{2,10},{6,14},... | collective-permute-start | bytes 3145736 | tf_op jit(solution)/shard_map/ppermute | solution.py:743
  224.6 61.4 %collective-permute-start.21 = (bf16[512,2048]{1,0:T(8,128)(2,1)}, bf16[512,2048]{1,0:T(8,128)(2,1)}, u32[]{:S(2)}, u32[]{:S(2)}) collective-permute-start(bf16[512,2048]{1,0:T(8,128)(2,1)} %get-tuple-element.125), channel_id=1, source_target_pairs={{0,16},{16,0},{1,17},{17,1},{2,18},{18,2},{3,19},{19,3},{4,20},{20... | collective-permute-start | bytes 6291464 | tf_op jit(solution)/shard_map/ppermute | solution.py:743
  246.7 28.9 %collective-permute-start.26 = (bf16[256,256]{1,0:T(8,128)(2,1)S(1)}, bf16[256,256]{1,0:T(8,128)(2,1)S(1)}, u32[]{:S(2)}, u32[]{:S(2)}) collective-permute-start(bf16[256,256]{1,0:T(8,128)(2,1)S(1)} %get-tuple-element.129), channel_id=1, source_target_pairs={{0,8},{8,0},{12,4},{1,9},{9,1},{13,5},{2,10},{10,2},{14,6},{3,11},... | collective-permute-start | bytes 393224 | tf_op jit(solution)/shard_map/ppermute | solution.py:991
  275.6 61.8 %collective-permute-start.36 = (bf16[256,2048]{1,0:T(8,128)(2,1)}, bf16[256,2048]{1,0:T(8,128)(2,1)S(1)}, u32[]{:S(2)}, u32[]{:S(2)}) collective-permute-start(bf16[256,2048]{1,0:T(8,128)(2,1)} %get-tuple-element.153), channel_id=1, source_target_pairs={{0,8},{4,12},{8,0},{12,4},{1,9},{5,13},{9,1},{13,5},{2,10},{6,14},... | collective-permute-start | bytes 3145736 | tf_op jit(solution)/shard_map/ppermute | solution.py:743
  279.4 43.5 %collective-permute-start.33 = (bf16[512,768]{1,0:T(8,128)(2,1)S(1)}, bf16[512,768]{1,0:T(8,128)(2,1)S(1)}, u32[]{:S(2)}, u32[]{:S(2)}) collective-permute-start(bf16[512,768]{1,0:T(8,128)(2,1)S(1)} %get-tuple-element.148.refs_13_.refs_15_), channel_id=1, source_target_pairs={{0,4},{4,0},{8,12},{12,8},{1,5},{5,1},{9,13},{13,9},{2,6},{6,2},{1... | collective-permute-start | bytes 2359304 | tf_op jit(solution)/shard_map/ppermute | solution.py:743
  299.1 63.6 %collective-permute-start.34 = (bf16[1024,512]{1,0:T(8,128)(2,1)}, bf16[1024,512]{1,0:T(8,128)(2,1)}, u32[]{:S(2)}, u32[]{:S(2)}) collective-permute-start(bf16[1024,512]{1,0:T(8,128)(2,1)} %get-tuple-element.151), channel_id=1, source_target_pairs={{0,4},{4,0},{8,12},{12,8},{1,5},{5,1},{9,13},{13,9},{2,6},{6,2},{1... | collective-permute-start | bytes 3145736 | tf_op jit(solution)/shard_map/ppermute | solution.py:743
  300.8 78.0 %collective-permute-start.40 = (bf16[256,2048]{1,0:T(8,128)(2,1)}, bf16[256,2048]{1,0:T(8,128)(2,1)}, u32[]{:S(2)}, u32[]{:S(2)}) collective-permute-start(bf16[256,2048]{1,0:T(8,128)(2,1)} %get-tuple-element.158), channel_id=1, source_target_pairs={{0,8},{4,12},{8,0},{12,4},{1,9},{5,13},{9,1},{13,5},{2,10},{6,14},... | collective-permute-start | bytes 3145736 | tf_op jit(solution)/shard_map/ppermute | solution.py:743
  330.1 20.2 %collective-permute-start.35 = (bf16[512,768]{1,0:T(8,128)(2,1)}, bf16[512,768]{1,0:T(8,128)(2,1)}, u32[]{:S(2)}, u32[]{:S(2)}) collective-permute-start(bf16[512,768]{1,0:T(8,128)(2,1)} %get-tuple-element.152), channel_id=1, source_target_pairs={{0,16},{16,0},{1,17},{17,1},{2,18},{18,2},{3,19},{19,3},{4,20},{20... | collective-permute-start | bytes 2359304 | tf_op jit(solution)/shard_map/ppermute | solution.py:743
  335.5 21.9 %collective-permute-start.30 = (bf16[128,2048]{1,0:T(8,128)(2,1)}, bf16[128,2048]{1,0:T(8,128)(2,1)S(1)}, u32[]{:S(2)}, u32[]{:S(2)}) collective-permute-start(bf16[128,2048]{1,0:T(8,128)(2,1)} %copy-done.38), channel_id=1, source_target_pairs={{0,1},{1,0},{2,3},{3,2},{4,5},{5,4},{6,7},{7,6},{8,9},{9,8},{10,11... | collective-permute-start | bytes 1572872 | tf_op jit(solution)/shard_map/ppermute | solution.py:743
  337.4 23.5 %collective-permute-start.32 = (bf16[128,2048]{1,0:T(8,128)(2,1)S(1)}, bf16[128,2048]{1,0:T(8,128)(2,1)S(1)}, u32[]{:S(2)}, u32[]{:S(2)}) collective-permute-start(bf16[128,2048]{1,0:T(8,128)(2,1)S(1)} %add_convert_fusion), channel_id=1, source_target_pairs={{0,2},{1,3},{2,0},{3,1},{4,6},{5,7},{6,4},{7,5},{8,10},{9,11},{10,... | collective-permute-start | bytes 1572872 | tf_op jit(solution)/shard_map/ppermute | solution.py:743
  357.3 34.2 %collective-permute-start.44 = (bf16[256,768]{1,0:T(8,128)(2,1)S(1)}, bf16[256,768]{1,0:T(8,128)(2,1)S(1)}, u32[]{:S(2)}, u32[]{:S(2)}) collective-permute-start(bf16[256,768]{1,0:T(8,128)(2,1)S(1)} %get-tuple-element.163), channel_id=1, source_target_pairs={{0,8},{4,12},{8,0},{12,4},{1,9},{5,13},{9,1},{13,5},{2,10},{6,14},... | collective-permute-start | bytes 1179656 | tf_op jit(solution)/shard_map/ppermute | solution.py:743
  385.2 15.4 %collective-permute-start.45 = (bf16[256,512]{1,0:T(8,128)(2,1)S(1)}, bf16[256,512]{1,0:T(8,128)(2,1)S(1)}, u32[]{:S(2)}, u32[]{:S(2)}) collective-permute-start(bf16[256,512]{1,0:T(8,128)(2,1)S(1)} %get-tuple-element.165), channel_id=1, source_target_pairs={{0,8},{4,12},{8,0},{12,4},{1,9},{5,13},{9,1},{13,5},{2,10},{6,14},... | collective-permute-start | bytes 786440 | tf_op jit(solution)/shard_map/ppermute | solution.py:743
  (96 other events, 988.7 us)
Sparse Core Ops, SparseCore 0:
  35.3 42.1 all-gather.1
  322.9 37.3 reduce-scatter.1

commit v2 on v1

--- a/solution.py
+++ b/solution.py
@@ -72,7 +72,7 @@
 class Chain:
     def __init__(self):
         self.held = []
-        self.cost = 58 * 10**8
+        self.cost = 69 * 10**8
         self.room = VMEM_BYTES // 2
 
     def wait(self, *arrays):
@@ -962,6 +962,7 @@
     normed_ffn_local = rms_norm(hidden_state, ffn_gain).astype(BF16)
     normed_ffn = tp_gather(normed_ffn_local)
     chain.room = 52 * 1024 * 1024
+    chain.cost = 58 * 10**8
     act, slope, silu = ffn_front(chain, normed_ffn, w_gate, w_up)
     normed_ffn_pair = tp_gather(flip(normed_ffn_local, "ctx", 1), chain.zero)
     act_pair, slope_pair, silu_pair = ffn_front(chain, normed_ffn_pair, w_gate, w_up)

time: 417 us -> 413 us (level)
  starting transfers between devices: 81.3 us -> 75.5 us
    ppermute x40, starting transfers between devices: 52 us -> 46.2 us  [flip(): return lax.ppermute(values_in, axis, [(i, i ^ mask) for i in range(count)])]
  transfers between devices with their start and end apart: 48 -> 48, of which waited for: 20 -> 21; matrix products, arithmetic and copies ran while one was open for 9% -> 9% of each run, Pallas kernels for 39% -> 39%
where the time goes in v2:
time: 413 us; the launch traced here: 408 us
  Pallas kernels  166 us (40%)
  waiting for transfers between devices  88 us (21%)
  starting transfers between devices  75.5 us (18%)
  other arithmetic  32.1 us (8%)
  local copies, waits for them, and re-layouts  28.7 us (7%)
  between operations  17.2 us (4%)
    pallas_call x23, Pallas kernels, call(): pl.pallas_call(inner, grid_spec=pltpu.PrefetchScalarGridSpec(num_scalar_p...  166 us
    ppermute x40, waiting for transfers between devices, flip(): return lax.ppermute(values_in, axis, [(i, i ^ mask) for i in range(count)])  80.7 us
    ppermute x40, starting transfers between devices, flip(): return lax.ppermute(values_in, axis, [(i, i ^ mask) for i in range(count)])  46.2 us
    unnamed x146, local copies, waits for them, and re-layouts  23.8 us
    ppermute x3, starting transfers between devices, per_device(): lax.ppermute(part, 'ctx', [(target, source) for source, target in moves])  20.5 us
    ppermute x3, starting transfers between devices, per_device(): tiles.append(lax.ppermute(held, 'ctx', moves))  8.82 us
  transfers between devices with their start and end apart: 48, of which 21 were waited for; matrix products, arithmetic and copies ran while one was open for 9% of the time, Pallas kernels for 39%

profile of v2, /device:TPU:0, one launch (start us, length us, event | category | flops | bytes accessed | tf_op | source)
XLA Modules:
  0.0 407.8 jit_solution(9621145077796337132)
XLA Ops:
  20.2 8.1 %collective-permute-done.1.refs_2_.refs_7_.refs_9_ = bf16[128,2048]{1,0:T(8,128)(2,1)S(1)} collective-permute-done((bf16[128,2048]{1,0:T(8,128)(2,1)S(1)}, bf16[128,2048]{1,0:T(8,128)(2,1)S(1)}, u32[]{:S(2)}, u32[]{:S(2)}) %collective-permute-start.1) | collective-permute-done | bytes 524320 | tf_op jit(solution)/shard_map/ppermute | solution.py:743
  56.8 7.3 %attend.1 = (bf16[512,512]{1,0:T(8,128)(2,1)S(1)}, f32[4,1,1024]{2,1,0:T(1,128)S(1)}, f32[8,128]{1,0:T(8,128)S(1)}) custom-call(bf16[512,256]{1,0:T(8,128)(2,1)S(1)} %collective-permute-done.3.refs_0_.refs_7_.refs_13_, bf16[256,256]{1,0:T(8,128)(2,1)S(1)} %collective-permute-done.4.refs_1_.refs_8_.refs_14_, ...), custom_call_target="tpu_custom_call" | custom-call | flops 6899999744 | bytes 1 | tf_op jit(solution)/shard_map/attend/pallas_call | solution.py:97
  70.1 16.8 %collective-permute-done.8 = bf16[128,2048]{1,0:T(8,128)(2,1)S(1)} collective-permute-done((bf16[128,2048]{1,0:T(8,128)(2,1)S(1)}, bf16[128,2048]{1,0:T(8,128)(2,1)S(1)}, u32[]{:S(2)}, u32[]{:S(2)}) %collective-permute-start.8) | collective-permute-done | bytes 524320 | tf_op jit(solution)/shard_map/ppermute | solution.py:743
  89.7 11.6 %collective-permute-done.10.refs_3_.refs_7_.refs_9_.refs_8_ = bf16[128,2048]{1,0:T(8,128)(2,1)S(1)} collective-permute-done((bf16[128,2048]{1,0:T(8,128)(2,1)S(1)}, bf16[128,2048]{1,0:T(8,128)(2,1)S(1)}, u32[]{:S(2)}, u32[]{:S(2)}) %collective-permute-start.10) | collective-permute-done | bytes 524320 | tf_op jit(solution)/shard_map/ppermute | solution.py:743
  103.3 14.4 %ffn_front.2 = (bf16[512,2048]{1,0:T(8,128)(2,1)}, bf16[512,2048]{1,0:T(8,128)(2,1)}, bf16[512,2048]{1,0:T(8,128)(2,1)}, f32[8,128]{1,0:T(8,128)S(1)}, f32[1,1]{1,0:T(1,128)}) custom-call(f32[8,128]{1,0:T(8,128)S(1)} %get-tuple-element.99.refs_0_, bf16[128,2048]{1,0:T(8,128)(2,1)S(1)} %multiply_convert_fusion.refs_1_.refs_5_.refs_7_.refs_6_, ...), custom_call_target="tpu_custom_call" | custom-call | flops 5800000000 | bytes 1 | tf_op jit(solution)/shard_map/ffn_front/pallas_call | solution.py:97
  122.2 14.6 %ffn_front.3 = (bf16[512,2048]{1,0:T(8,128)(2,1)}, bf16[512,2048]{1,0:T(8,128)(2,1)}, bf16[512,2048]{1,0:T(8,128)(2,1)}, f32[8,128]{1,0:T(8,128)S(1)}, f32[1,1]{1,0:T(1,128)}) custom-call(f32[8,128]{1,0:T(8,128)S(1)} %get-tuple-element.100.refs_0_, bf16[128,2048]{1,0:T(8,128)(2,1)} %collective-permute-done.12.refs_1_.refs_9_.refs_11_.refs_10_, ...), custom_call_target="tpu_custom_call" | custom-call | flops 5800000000 | bytes 1 | tf_op jit(solution)/shard_map/ffn_front/pallas_call | solution.py:97
  136.8 6.8 %weight_terms.8 = (bf16[512,2048]{1,0:T(8,128)(2,1)}, f32[8,128]{1,0:T(8,128)S(1)}) custom-call(s32[2]{0:T(128)S(1)} %add_add_fusion.5.refs_0_.refs_1_, s32[2]{0:T(128)S(1)} %add_add_fusion.5.refs_0_.refs_1_, s32[4]{0:T(128)S(1)} %iota_xor_fusion.1.refs_2_.refs_0_.refs_3_.refs_1_, f32[8,128]{1,0:T(8,128)S(1)} %get-tuple-element.102.refs_3_, ...), custom_call_target="tpu_custom_call" | custom-call | flops 5800000000 | bytes 1 | tf_op jit(solution)/shard_map/weight_terms/pallas_call | solution.py:97
  145.1 10.9 %ffn_back.2 = (bf16[512,2048]{1,0:T(8,128)(2,1)}, bf16[512,2048]{1,0:T(8,128)(2,1)}, f32[8,128]{1,0:T(8,128)S(1)}) custom-call(s32[4]{0:T(128)S(1)} %iota_xor_fusion.1.refs_2_.refs_0_.refs_3_.refs_1_, f32[8,128]{1,0:T(8,128)S(1)} %get-tuple-element.105.refs_1_, ...), custom_call_target="tpu_custom_call" | custom-call | flops 5800000000 | bytes 1 | tf_op jit(solution)/shard_map/ffn_back/pallas_call | solution.py:97
  156.0 14.9 %pull.4 = (bf16[128,2048]{1,0:T(8,128)(2,1)S(1)}, bf16[128,2048]{1,0:T(8,128)(2,1)S(1)}, bf16[128,2048]{1,0:T(8,128)(2,1)S(1)}, bf16[128,2048]{1,0:T(8,128)(2,1)}, f32[8,128]{1,0:T(8,128)S(1)}, /*index=5*/f32[1,1]{1,0:T(1,128)}) custom-call(f32[8,128]{1,0:T(8,128)S(1)} %get-tuple-element.108.refs_0_, ...), custom_call_target="tpu_custom_call" | custom-call | flops 5800000000 | bytes 1 | tf_op jit(solution)/shard_map/pull/pallas_call | solution.py:97
  171.5 10.9 %ffn_back.3 = (bf16[512,2048]{1,0:T(8,128)(2,1)}, bf16[512,2048]{1,0:T(8,128)(2,1)}, f32[8,128]{1,0:T(8,128)S(1)}) custom-call(s32[4]{0:T(128)S(1)} %iota_xor_fusion.1.refs_2_.refs_0_.refs_3_.refs_1_, f32[8,128]{1,0:T(8,128)S(1)} %get-tuple-element.116.refs_1_, ...), custom_call_target="tpu_custom_call" | custom-call | flops 5800000000 | bytes 1 | tf_op jit(solution)/shard_map/ffn_back/pallas_call | solution.py:97
  183.1 6.8 %weight_terms.9 = (bf16[512,2048]{1,0:T(8,128)(2,1)}, f32[8,128]{1,0:T(8,128)S(1)}) custom-call(s32[2]{0:T(128)S(1)} %add_add_fusion.5.refs_0_.refs_1_, s32[2]{0:T(128)S(1)} %add_add_fusion.5.refs_0_.refs_1_, s32[4]{0:T(128)S(1)} %iota_xor_fusion.1.refs_2_.refs_0_.refs_3_.refs_1_, bf16[128,2048]{1,0:T(8,128)(2,1)S(1)} %add_convert_fusion.2.refs_3_, ...), custom_call_target="tpu_custom_call" | custom-call | flops 5800000000 | bytes 1 | tf_op jit(solution)/shard_map/weight_terms/pallas_call | solution.py:97
  193.1 7.8 %weight_terms.10 = (bf16[256,2048]{1,0:T(8,128)(2,1)}, bf16[256,2048]{1,0:T(8,128)(2,1)}, f32[8,128]{1,0:T(8,128)S(1)}, f32[1,1]{1,0:T(1,128)}) custom-call(s32[2]{0:T(128)S(1)} %and_select_fusion.1.refs_0_, s32[2]{0:T(128)S(1)} %gather_fusion, s32[2]{0:T(128)S(1)} %gather_fusion, s32[4]{0:T(128)S(1)} %iota_xor_fusion.1.refs_2_.refs_0_.refs_3_.refs_1_, ...), custom_call_target="tpu_custom_call" | custom-call | flops 5800000000 | bytes 1 | tf_op jit(solution)/shard_map/weight_terms/pallas_call | solution.py:97
  204.6 9.5 %collective-permute-start.29 = (bf16[256,2048]{1,0:T(8,128)(2,1)}, bf16[256,2048]{1,0:T(8,128)(2,1)S(1)}, u32[]{:S(2)}, u32[]{:S(2)}) collective-permute-start(bf16[256,2048]{1,0:T(8,128)(2,1)} %get-tuple-element.132), channel_id=1, source_target_pairs={{0,8},{4,12},{8,0},{12,4},{1,9},{5,13},{9,1},{13,5},{2,10},{6,14},... | collective-permute-start | bytes 3145736 | tf_op jit(solution)/shard_map/ppermute | solution.py:743
  214.1 6.8 %weight_terms.11 = (bf16[512,2048]{1,0:T(8,128)(2,1)}, f32[8,128]{1,0:T(8,128)S(1)}) custom-call(s32[2]{0:T(128)S(1)} %add_add_fusion.5.refs_0_.refs_1_, s32[2]{0:T(128)S(1)} %add_add_fusion.5.refs_0_.refs_1_, s32[4]{0:T(128)S(1)} %iota_xor_fusion.1.refs_2_.refs_0_.refs_3_.refs_1_, bf16[128,2048]{1,0:T(8,128)(2,1)S(1)} %get-tuple-element.208.refs_3_.refs_8_.refs_5_, ...), custom_call_target="tpu_custom_call" | custom-call | flops 5800000000 | bytes 1 | tf_op jit(solution)/shard_map/weight_terms/pallas_call | solution.py:97
  227.6 15.3 %attend_back.1 = (bf16[512,512]{1,0:T(8,128)(2,1)}, f32[512,256]{1,0:T(8,128)}, bf16[512,256]{1,0:T(8,128)(2,1)S(1)}, bf16[256,256]{1,0:T(8,128)(2,1)S(1)}, bf16...) custom-call(f32[8,128]{1,0:T(8,128)S(1)} %get-tuple-element.126.refs_0_, s32[16]{0:T(128)S(1)} %concatenate.33.refs_4_.refs_1_, ...), custom_call_target="tpu_custom_call" | custom-call | flops 5800000000 | bytes 1 | tf_op jit(solution)/shard_map/attend_back/pallas_call | solution.py:97
  243.0 16.5 %collective-permute-start.26 = (bf16[256,256]{1,0:T(8,128)(2,1)S(1)}, bf16[256,256]{1,0:T(8,128)(2,1)S(1)}, u32[]{:S(2)}, u32[]{:S(2)}) collective-permute-start(bf16[256,256]{1,0:T(8,128)(2,1)S(1)} %get-tuple-element.129), channel_id=1, source_target_pairs={{0,8},{8,0},{12,4},{1,9},{9,1},{13,5},{2,10},{10,2},{14,6},{3,11},... | collective-permute-start | bytes 393224 | tf_op jit(solution)/shard_map/ppermute | solution.py:992
  263.5 7.4 %weight_terms.12 = (bf16[256,2048]{1,0:T(8,128)(2,1)}, bf16[256,2048]{1,0:T(8,128)(2,1)S(1)}, f32[8,128]{1,0:T(8,128)S(1)}, f32[1,1]{1,0:T(1,128)}) custom-call(s32[2]{0:T(128)S(1)} %and_select_fusion.1.refs_0_, s32[2]{0:T(128)S(1)} %gather_fusion, s32[2]{0:T(128)S(1)} %gather_fusion, s32[4]{0:T(128)S(1)} %iota_xor_fusion.1.refs_2_.refs_0_.refs_3_.refs_1_, ...), custom_call_target="tpu_custom_call" | custom-call | flops 5800000000 | bytes 1 | tf_op jit(solution)/shard_map/weight_terms/pallas_call | solution.py:97
  277.2 5.3 %collective-permute-done.21.refs_4_.refs_16_ = bf16[512,2048]{1,0:T(8,128)(2,1)} collective-permute-done((bf16[512,2048]{1,0:T(8,128)(2,1)}, bf16[512,2048]{1,0:T(8,128)(2,1)}, u32[]{:S(2)}, u32[]{:S(2)}) %collective-permute-start.21) | collective-permute-done | bytes 2097184 | tf_op jit(solution)/shard_map/ppermute | solution.py:743
  282.5 7.2 %weight_terms.13 = (bf16[256,2048]{1,0:T(8,128)(2,1)}, bf16[256,2048]{1,0:T(8,128)(2,1)S(1)}, f32[8,128]{1,0:T(8,128)S(1)}, f32[1,1]{1,0:T(1,128)}) custom-call(s32[2]{0:T(128)S(1)} %and_select_fusion.1.refs_0_, s32[2]{0:T(128)S(1)} %gather_fusion, s32[2]{0:T(128)S(1)} %gather_fusion, s32[4]{0:T(128)S(1)} %iota_xor_fusion.1.refs_2_.refs_0_.refs_3_.refs_1_, ...), custom_call_target="tpu_custom_call" | custom-call | flops 5800000000 | bytes 1 | tf_op jit(solution)/shard_map/weight_terms/pallas_call | solution.py:97
  290.7 4.8 %own_terms.2 = (bf16[1024,512]{1,0:T(8,128)(2,1)}, f32[8,128]{1,0:T(8,128)S(1)}, f32[1,1]{1,0:T(1,128)}) custom-call(s32[4]{0:T(128)S(1)} %fusion.22.refs_0_, s32[4]{0:T(128)S(1)} %iota_xor_fusion.1.refs_2_.refs_0_.refs_3_.refs_1_, f32[8,128]{1,0:T(8,128)S(1)} %get-tuple-element.138.refs_2_, bf16[128,2048]{1,0:T(8,128)(2,1)S(1)} %copy-done.25, ...), custom_call_target="tpu_custom_call" | custom-call | flops 5800000000 | bytes 1 | tf_op jit(solution)/shard_map/own_terms/pallas_call | solution.py:97
  297.0 9.5 %collective-permute-start.40 = (bf16[256,2048]{1,0:T(8,128)(2,1)}, bf16[256,2048]{1,0:T(8,128)(2,1)}, u32[]{:S(2)}, u32[]{:S(2)}) collective-permute-start(bf16[256,2048]{1,0:T(8,128)(2,1)} %get-tuple-element.158), channel_id=1, source_target_pairs={{0,8},{4,12},{8,0},{12,4},{1,9},{5,13},{9,1},{13,5},{2,10},{6,14},... | collective-permute-start | bytes 3145736 | tf_op jit(solution)/shard_map/ppermute | solution.py:743
  309.8 7.7 %push.1 = (bf16[512,2048]{1,0:T(8,128)(2,1)S(1)}, f32[8,128]{1,0:T(8,128)S(1)}) custom-call(s32[4]{0:T(128)S(1)} %iota_xor_fusion.1.refs_2_.refs_0_.refs_3_.refs_1_, f32[8,128]{1,0:T(8,128)S(1)} %get-tuple-element.142.refs_1_, bf16[512,2048]{1,0:T(8,128)(2,1)S(1)} %copy-done, bf16[2048,2048]{1,0:T(8,128)(2,1)} %refs_3_.3), custom_call_target="tpu_custom_call" | custom-call | flops 5800000000 | bytes 1 | tf_op jit(solution)/shard_map/push/pallas_call | solution.py:97
  334.1 12.5 %collective-permute-done.35.refs_4_.refs_17_ = bf16[512,768]{1,0:T(8,128)(2,1)} collective-permute-done((bf16[512,768]{1,0:T(8,128)(2,1)}, bf16[512,768]{1,0:T(8,128)(2,1)}, u32[]{:S(2)}, u32[]{:S(2)}) %collective-permute-start.35) | collective-permute-done | bytes 786464 | tf_op jit(solution)/shard_map/ppermute | solution.py:743
  359.1 4.5 %own_terms.3 = (bf16[512,512]{1,0:T(8,128)(2,1)S(1)}, bf16[512,512]{1,0:T(8,128)(2,1)S(1)}, f32[8,128]{1,0:T(8,128)S(1)}, f32[1,1]{1,0:T(1,128)}) custom-call(s32[4]{0:T(128)S(1)} %get-tuple-element.207.refs_0_, s32[4]{0:T(128)S(1)} %get-tuple-element.206.refs_1_, s32[4]{0:T(128)S(1)} %iota_xor_fusion.1.refs_2_.refs_0_.refs_3_.refs_1_, ...), custom_call_target="tpu_custom_call" | custom-call | flops 5800000000 | bytes 1 | tf_op jit(solution)/shard_map/own_terms/pallas_call | solution.py:97
  (301 shorter events, 152.8 us)
Async XLA Ops:
  7.2 129.7 %all-gather.2.cloned.1.call-start = ((), (), s32[]{:S(2)}) async-start(), calls=%async_computation.1 | async-start | bytes 6553600 | tf_op jit(solution)/shard_map/all_gather | solution.py:942
  11.9 20.9 %collective-permute-start.16 = (bf16[128,3072]{1,0:T(8,128)(2,1)}, bf16[128,3072]{1,0:T(8,128)(2,1)}, u32[]{:S(2)}, u32[]{:S(2)}) collective-permute-start(bf16[128,3072]{1,0:T(8,128)(2,1)} %pad_maximum_fusion.1), channel_id=1, source_target_pairs={{0,4},{4,0},{8,12},{12,8},{1,5},{5,1},{9,13},{13,9},{2,6},{6,2},{1... | collective-permute-start | bytes 2359304 | tf_op jit(solution)/shard_map/ppermute | solution.py:743
  16.4 18.9 %collective-permute-start = (bf16[128,2048]{1,0:T(8,128)(2,1)S(1)}, bf16[128,2048]{1,0:T(8,128)(2,1)S(1)}, u32[]{:S(2)}, u32[]{:S(2)}) collective-permute-start(bf16[128,2048]{1,0:T(8,128)(2,1)S(1)} %fusion.2.refs_0_.refs_5_.refs_7_), channel_id=1, source_target_pairs={{0,1},{1,0},{2,3},{3,2},{4,5},{5,4},{6,7},{7,6},{8,9},{9,8},{10,11... | collective-permute-start | bytes 1572872 | tf_op jit(solution)/shard_map/ppermute | solution.py:743
  35.3 363.6 %reduce-scatter.2.cloned.1.call-start = ((), (), s32[]{:S(2)}) async-start(), calls=%async_computation.2 | async-start | bytes 2621440 | tf_op jit(solution)/shard_map/reduce_scatter | solution.py:1005
  68.5 18.4 %collective-permute-start.8 = (bf16[128,2048]{1,0:T(8,128)(2,1)S(1)}, bf16[128,2048]{1,0:T(8,128)(2,1)S(1)}, u32[]{:S(2)}, u32[]{:S(2)}) collective-permute-start(bf16[128,2048]{1,0:T(8,128)(2,1)S(1)} %add_convert_fusion.4), channel_id=1, source_target_pairs={{0,2},{1,3},{2,0},{3,1},{4,6},{5,7},{6,4},{7,5},{8,10},{9,11},{10,... | collective-permute-start | bytes 1572872 | tf_op jit(solution)/shard_map/ppermute | solution.py:743
  101.5 16.2 %collective-permute-start.14 = (bf16[128,2048]{1,0:T(8,128)(2,1)}, bf16[128,2048]{1,0:T(8,128)(2,1)S(1)}, u32[]{:S(2)}, u32[]{:S(2)}) collective-permute-start(bf16[128,2048]{1,0:T(8,128)(2,1)} %collective-permute-done.12.refs_1_.refs_9_.refs_11_.refs_10_), channel_id=1, source_target_pairs={{0,2},{1,3},{2,0},{3,1},{4,6},{5,7},{6,4},{7,5},{8,10},{9,11},{10,... | collective-permute-start | bytes 1572872 | tf_op jit(solution)/shard_map/ppermute | solution.py:743
  103.1 17.2 %collective-permute-start.13 = (bf16[128,2048]{1,0:T(8,128)(2,1)}, bf16[128,2048]{1,0:T(8,128)(2,1)}, u32[]{:S(2)}, u32[]{:S(2)}) collective-permute-start(bf16[128,2048]{1,0:T(8,128)(2,1)} %collective-permute-done.12.refs_1_.refs_9_.refs_11_.refs_10_), channel_id=1, source_target_pairs={{0,1},{1,0},{2,3},{3,2},{4,5},{5,4},{6,7},{7,6},{8,9},{9,8},{10,11... | collective-permute-start | bytes 1572872 | tf_op jit(solution)/shard_map/ppermute | solution.py:743
  143.7 48.1 %collective-permute-start.20 = (bf16[512,2048]{1,0:T(8,128)(2,1)}, bf16[512,2048]{1,0:T(8,128)(2,1)S(1)}, u32[]{:S(2)}, u32[]{:S(2)}) collective-permute-start(bf16[512,2048]{1,0:T(8,128)(2,1)} %get-tuple-element.115), channel_id=1, source_target_pairs={{0,16},{16,0},{1,17},{17,1},{2,18},{18,2},{3,19},{19,3},{4,20},{20... | collective-permute-start | bytes 6291464 | tf_op jit(solution)/shard_map/ppermute | solution.py:743
  170.9 29.9 %collective-permute-start.17 = (bf16[128,2048]{1,0:T(8,128)(2,1)S(1)}, bf16[128,2048]{1,0:T(8,128)(2,1)S(1)}, u32[]{:S(2)}, u32[]{:S(2)}) collective-permute-start(bf16[128,2048]{1,0:T(8,128)(2,1)S(1)} %get-tuple-element.112), channel_id=1, source_target_pairs={{0,1},{1,0},{2,3},{3,2},{4,5},{5,4},{6,7},{7,6},{8,9},{9,8},{10,11... | collective-permute-start | bytes 1572872 | tf_op jit(solution)/shard_map/ppermute | solution.py:743
  182.5 18.4 %collective-permute-start.19 = (bf16[128,2048]{1,0:T(8,128)(2,1)S(1)}, bf16[128,2048]{1,0:T(8,128)(2,1)S(1)}, u32[]{:S(2)}, u32[]{:S(2)}) collective-permute-start(bf16[128,2048]{1,0:T(8,128)(2,1)S(1)} %add_convert_fusion.2.refs_3_), channel_id=1, source_target_pairs={{0,2},{1,3},{2,0},{3,1},{4,6},{5,7},{6,4},{7,5},{8,10},{9,11},{10,... | collective-permute-start | bytes 1572872 | tf_op jit(solution)/shard_map/ppermute | solution.py:743
  189.9 70.8 %collective-permute-start.28 = (bf16[512,2048]{1,0:T(8,128)(2,1)}, bf16[512,2048]{1,0:T(8,128)(2,1)}, u32[]{:S(2)}, u32[]{:S(2)}) collective-permute-start(bf16[512,2048]{1,0:T(8,128)(2,1)} %get-tuple-element.131), channel_id=1, source_target_pairs={{0,16},{16,0},{1,17},{17,1},{2,18},{18,2},{3,19},{19,3},{4,20},{20... | collective-permute-start | bytes 6291464 | tf_op jit(solution)/shard_map/ppermute | solution.py:743
  204.3 18.4 %collective-permute-start.23 = (bf16[128,2048]{1,0:T(8,128)(2,1)S(1)}, bf16[128,2048]{1,0:T(8,128)(2,1)}, u32[]{:S(2)}, u32[]{:S(2)}) collective-permute-start(bf16[128,2048]{1,0:T(8,128)(2,1)S(1)} %get-tuple-element.208.refs_3_.refs_8_.refs_5_), channel_id=1, source_target_pairs={{0,2},{1,3},{2,0},{3,1},{4,6},{5,7},{6,4},{7,5},{8,10},{9,11},{10,... | collective-permute-start | bytes 1572872 | tf_op jit(solution)/shard_map/ppermute | solution.py:743
  204.6 18.8 %collective-permute-start.22 = (bf16[128,2048]{1,0:T(8,128)(2,1)S(1)}, bf16[128,2048]{1,0:T(8,128)(2,1)}, u32[]{:S(2)}, u32[]{:S(2)}) collective-permute-start(bf16[128,2048]{1,0:T(8,128)(2,1)S(1)} %get-tuple-element.208.refs_3_.refs_8_.refs_5_), channel_id=1, source_target_pairs={{0,1},{1,0},{2,3},{3,2},{4,5},{5,4},{6,7},{7,6},{8,9},{9,8},{10,11... | collective-permute-start | bytes 1572872 | tf_op jit(solution)/shard_map/ppermute | solution.py:743
  204.6 58.8 %collective-permute-start.29 = (bf16[256,2048]{1,0:T(8,128)(2,1)}, bf16[256,2048]{1,0:T(8,128)(2,1)S(1)}, u32[]{:S(2)}, u32[]{:S(2)}) collective-permute-start(bf16[256,2048]{1,0:T(8,128)(2,1)} %get-tuple-element.132), channel_id=1, source_target_pairs={{0,8},{4,12},{8,0},{12,4},{1,9},{5,13},{9,1},{13,5},{2,10},{6,14},... | collective-permute-start | bytes 3145736 | tf_op jit(solution)/shard_map/ppermute | solution.py:743
  220.9 61.6 %collective-permute-start.21 = (bf16[512,2048]{1,0:T(8,128)(2,1)}, bf16[512,2048]{1,0:T(8,128)(2,1)}, u32[]{:S(2)}, u32[]{:S(2)}) collective-permute-start(bf16[512,2048]{1,0:T(8,128)(2,1)} %get-tuple-element.125), channel_id=1, source_target_pairs={{0,16},{16,0},{1,17},{17,1},{2,18},{18,2},{3,19},{19,3},{4,20},{20... | collective-permute-start | bytes 6291464 | tf_op jit(solution)/shard_map/ppermute | solution.py:743
  243.0 28.9 %collective-permute-start.26 = (bf16[256,256]{1,0:T(8,128)(2,1)S(1)}, bf16[256,256]{1,0:T(8,128)(2,1)S(1)}, u32[]{:S(2)}, u32[]{:S(2)}) collective-permute-start(bf16[256,256]{1,0:T(8,128)(2,1)S(1)} %get-tuple-element.129), channel_id=1, source_target_pairs={{0,8},{8,0},{12,4},{1,9},{9,1},{13,5},{2,10},{10,2},{14,6},{3,11},... | collective-permute-start | bytes 393224 | tf_op jit(solution)/shard_map/ppermute | solution.py:992
  271.9 61.8 %collective-permute-start.36 = (bf16[256,2048]{1,0:T(8,128)(2,1)}, bf16[256,2048]{1,0:T(8,128)(2,1)S(1)}, u32[]{:S(2)}, u32[]{:S(2)}) collective-permute-start(bf16[256,2048]{1,0:T(8,128)(2,1)} %get-tuple-element.153), channel_id=1, source_target_pairs={{0,8},{4,12},{8,0},{12,4},{1,9},{5,13},{9,1},{13,5},{2,10},{6,14},... | collective-permute-start | bytes 3145736 | tf_op jit(solution)/shard_map/ppermute | solution.py:743
  275.6 43.5 %collective-permute-start.33 = (bf16[512,768]{1,0:T(8,128)(2,1)S(1)}, bf16[512,768]{1,0:T(8,128)(2,1)S(1)}, u32[]{:S(2)}, u32[]{:S(2)}) collective-permute-start(bf16[512,768]{1,0:T(8,128)(2,1)S(1)} %get-tuple-element.148.refs_13_.refs_15_), channel_id=1, source_target_pairs={{0,4},{4,0},{8,12},{12,8},{1,5},{5,1},{9,13},{13,9},{2,6},{6,2},{1... | collective-permute-start | bytes 2359304 | tf_op jit(solution)/shard_map/ppermute | solution.py:743
  295.5 63.6 %collective-permute-start.34 = (bf16[1024,512]{1,0:T(8,128)(2,1)}, bf16[1024,512]{1,0:T(8,128)(2,1)}, u32[]{:S(2)}, u32[]{:S(2)}) collective-permute-start(bf16[1024,512]{1,0:T(8,128)(2,1)} %get-tuple-element.151), channel_id=1, source_target_pairs={{0,4},{4,0},{8,12},{12,8},{1,5},{5,1},{9,13},{13,9},{2,6},{6,2},{1... | collective-permute-start | bytes 3145736 | tf_op jit(solution)/shard_map/ppermute | solution.py:743
  297.0 78.0 %collective-permute-start.40 = (bf16[256,2048]{1,0:T(8,128)(2,1)}, bf16[256,2048]{1,0:T(8,128)(2,1)}, u32[]{:S(2)}, u32[]{:S(2)}) collective-permute-start(bf16[256,2048]{1,0:T(8,128)(2,1)} %get-tuple-element.158), channel_id=1, source_target_pairs={{0,8},{4,12},{8,0},{12,4},{1,9},{5,13},{9,1},{13,5},{2,10},{6,14},... | collective-permute-start | bytes 3145736 | tf_op jit(solution)/shard_map/ppermute | solution.py:743
  326.4 20.2 %collective-permute-start.35 = (bf16[512,768]{1,0:T(8,128)(2,1)}, bf16[512,768]{1,0:T(8,128)(2,1)}, u32[]{:S(2)}, u32[]{:S(2)}) collective-permute-start(bf16[512,768]{1,0:T(8,128)(2,1)} %get-tuple-element.152), channel_id=1, source_target_pairs={{0,16},{16,0},{1,17},{17,1},{2,18},{18,2},{3,19},{19,3},{4,20},{20... | collective-permute-start | bytes 2359304 | tf_op jit(solution)/shard_map/ppermute | solution.py:743
  331.7 21.9 %collective-permute-start.30 = (bf16[128,2048]{1,0:T(8,128)(2,1)}, bf16[128,2048]{1,0:T(8,128)(2,1)S(1)}, u32[]{:S(2)}, u32[]{:S(2)}) collective-permute-start(bf16[128,2048]{1,0:T(8,128)(2,1)} %copy-done.38), channel_id=1, source_target_pairs={{0,1},{1,0},{2,3},{3,2},{4,5},{5,4},{6,7},{7,6},{8,9},{9,8},{10,11... | collective-permute-start | bytes 1572872 | tf_op jit(solution)/shard_map/ppermute | solution.py:743
  333.6 23.6 %collective-permute-start.32 = (bf16[128,2048]{1,0:T(8,128)(2,1)S(1)}, bf16[128,2048]{1,0:T(8,128)(2,1)S(1)}, u32[]{:S(2)}, u32[]{:S(2)}) collective-permute-start(bf16[128,2048]{1,0:T(8,128)(2,1)S(1)} %add_convert_fusion), channel_id=1, source_target_pairs={{0,2},{1,3},{2,0},{3,1},{4,6},{5,7},{6,4},{7,5},{8,10},{9,11},{10,... | collective-permute-start | bytes 1572872 | tf_op jit(solution)/shard_map/ppermute | solution.py:743
  353.6 34.2 %collective-permute-start.44 = (bf16[256,768]{1,0:T(8,128)(2,1)S(1)}, bf16[256,768]{1,0:T(8,128)(2,1)S(1)}, u32[]{:S(2)}, u32[]{:S(2)}) collective-permute-start(bf16[256,768]{1,0:T(8,128)(2,1)S(1)} %get-tuple-element.163), channel_id=1, source_target_pairs={{0,8},{4,12},{8,0},{12,4},{1,9},{5,13},{9,1},{13,5},{2,10},{6,14},... | collective-permute-start | bytes 1179656 | tf_op jit(solution)/shard_map/ppermute | solution.py:743
  (96 other events, 971.5 us)
Sparse Core Ops, SparseCore 0:
  35.4 46.1 all-gather.1
  319.1 37.4 reduce-scatter.1

commit v3 on v2

--- a/solution.py
+++ b/solution.py
@@ -1015,7 +1015,7 @@
     qkv_w.keep()
     out_w.send()
     out_zero = chain.zero
-    chain.wait(up_w.received)
+    chain.wait(up_w.received, layer_out)
     out_w.keep()
     zero = chain.zero
     gains = sum_over(jnp.stack([grad_attn_gain, grad_ffn_gain]) + out_zero, "tp")

time: 413 us -> 420 us (1.017)
    unnamed x146 -> x166, local copies, waits for them, and re-layouts: 23.8 us -> 24.7 us
  transfers between devices with their start and end apart: 48 -> 48, of which waited for: 21 -> 20; matrix products, arithmetic and copies ran while one was open for 9% -> 9% of each run, Pallas kernels for 39% -> 38%
where the time goes in v3:
time: 420 us; the launch traced here: 414 us
  Pallas kernels  166 us (40%)
  waiting for transfers between devices  89.3 us (21%)
  starting transfers between devices  77.7 us (18%)
  other arithmetic  33.9 us (8%)
  local copies, waits for them, and re-layouts  30.1 us (7%)
  between operations  17.3 us (4%)
    pallas_call x23, Pallas kernels, call(): pl.pallas_call(inner, grid_spec=pltpu.PrefetchScalarGridSpec(num_scalar_p...  166 us
    ppermute x40, waiting for transfers between devices, flip(): return lax.ppermute(values_in, axis, [(i, i ^ mask) for i in range(count)])  81.9 us
    ppermute x40, starting transfers between devices, flip(): return lax.ppermute(values_in, axis, [(i, i ^ mask) for i in range(count)])  48.4 us
    unnamed x166, local copies, waits for them, and re-layouts  24.7 us
    ppermute x3, starting transfers between devices, per_device(): lax.ppermute(part, 'ctx', [(target, source) for source, target in moves])  20.4 us
    ppermute x3, starting transfers between devices, per_device(): tiles.append(lax.ppermute(held, 'ctx', moves))  8.82 us
  transfers between devices with their start and end apart: 48, of which 20 were waited for; matrix products, arithmetic and copies ran while one was open for 9% of the time, Pallas kernels for 38%

profile of v3, /device:TPU:0, one launch (start us, length us, event | category | flops | bytes accessed | tf_op | source)
XLA Modules:
  0.0 414.5 jit_solution(16525192962210163101)
XLA Ops:
  20.4 8.1 %collective-permute-done.1.refs_2_.refs_7_.refs_9_ = bf16[128,2048]{1,0:T(8,128)(2,1)S(1)} collective-permute-done((bf16[128,2048]{1,0:T(8,128)(2,1)S(1)}, bf16[128,2048]{1,0:T(8,128)(2,1)S(1)}, u32[]{:S(2)}, u32[]{:S(2)}) %collective-permute-start.1) | collective-permute-done | bytes 524320 | tf_op jit(solution)/shard_map/ppermute | solution.py:743
  57.0 7.3 %attend.1 = (bf16[512,512]{1,0:T(8,128)(2,1)S(1)}, f32[4,1,1024]{2,1,0:T(1,128)S(1)}, f32[8,128]{1,0:T(8,128)S(1)}) custom-call(bf16[512,256]{1,0:T(8,128)(2,1)S(1)} %collective-permute-done.3.refs_0_.refs_7_.refs_13_, bf16[256,256]{1,0:T(8,128)(2,1)S(1)} %collective-permute-done.4.refs_1_.refs_8_.refs_14_, ...), custom_call_target="tpu_custom_call" | custom-call | flops 6899999744 | bytes 1 | tf_op jit(solution)/shard_map/attend/pallas_call | solution.py:97
  70.3 16.8 %collective-permute-done.8 = bf16[128,2048]{1,0:T(8,128)(2,1)S(1)} collective-permute-done((bf16[128,2048]{1,0:T(8,128)(2,1)S(1)}, bf16[128,2048]{1,0:T(8,128)(2,1)S(1)}, u32[]{:S(2)}, u32[]{:S(2)}) %collective-permute-start.8) | collective-permute-done | bytes 524320 | tf_op jit(solution)/shard_map/ppermute | solution.py:743
  90.4 11.1 %collective-permute-done.10.refs_3_.refs_7_.refs_9_.refs_8_ = bf16[128,2048]{1,0:T(8,128)(2,1)S(1)} collective-permute-done((bf16[128,2048]{1,0:T(8,128)(2,1)S(1)}, bf16[128,2048]{1,0:T(8,128)(2,1)S(1)}, u32[]{:S(2)}, u32[]{:S(2)}) %collective-permute-start.10) | collective-permute-done | bytes 524320 | tf_op jit(solution)/shard_map/ppermute | solution.py:743
  103.5 14.4 %ffn_front.2 = (bf16[512,2048]{1,0:T(8,128)(2,1)}, bf16[512,2048]{1,0:T(8,128)(2,1)}, bf16[512,2048]{1,0:T(8,128)(2,1)}, f32[8,128]{1,0:T(8,128)S(1)}, f32[1,1]{1,0:T(1,128)}) custom-call(f32[8,128]{1,0:T(8,128)S(1)} %get-tuple-element.99.refs_0_, bf16[128,2048]{1,0:T(8,128)(2,1)S(1)} %multiply_convert_fusion.refs_1_.refs_5_.refs_7_.refs_6_, ...), custom_call_target="tpu_custom_call" | custom-call | flops 5800000000 | bytes 1 | tf_op jit(solution)/shard_map/ffn_front/pallas_call | solution.py:97
  122.4 14.5 %ffn_front.3 = (bf16[512,2048]{1,0:T(8,128)(2,1)}, bf16[512,2048]{1,0:T(8,128)(2,1)}, bf16[512,2048]{1,0:T(8,128)(2,1)}, f32[8,128]{1,0:T(8,128)S(1)}, f32[1,1]{1,0:T(1,128)}) custom-call(f32[8,128]{1,0:T(8,128)S(1)} %get-tuple-element.100.refs_0_, bf16[128,2048]{1,0:T(8,128)(2,1)S(1)} %collective-permute-done.12.refs_1_.refs_9_.refs_11_.refs_10_, ...), custom_call_target="tpu_custom_call" | custom-call | flops 5800000000 | bytes 1 | tf_op jit(solution)/shard_map/ffn_front/pallas_call | solution.py:97
  136.8 6.8 %weight_terms.8 = (bf16[512,2048]{1,0:T(8,128)(2,1)}, f32[8,128]{1,0:T(8,128)S(1)}) custom-call(s32[2]{0:T(128)S(1)} %add_add_fusion.5.refs_0_.refs_1_, s32[2]{0:T(128)S(1)} %add_add_fusion.5.refs_0_.refs_1_, s32[4]{0:T(128)S(1)} %iota_xor_fusion.1.refs_2_.refs_0_.refs_3_.refs_1_, f32[8,128]{1,0:T(8,128)S(1)} %get-tuple-element.102.refs_3_, ...), custom_call_target="tpu_custom_call" | custom-call | flops 5800000000 | bytes 1 | tf_op jit(solution)/shard_map/weight_terms/pallas_call | solution.py:97
  145.2 10.8 %ffn_back.2 = (bf16[512,2048]{1,0:T(8,128)(2,1)}, bf16[512,2048]{1,0:T(8,128)(2,1)}, f32[8,128]{1,0:T(8,128)S(1)}) custom-call(s32[4]{0:T(128)S(1)} %iota_xor_fusion.1.refs_2_.refs_0_.refs_3_.refs_1_, f32[8,128]{1,0:T(8,128)S(1)} %get-tuple-element.105.refs_1_, ...), custom_call_target="tpu_custom_call" | custom-call | flops 5800000000 | bytes 1 | tf_op jit(solution)/shard_map/ffn_back/pallas_call | solution.py:97
  156.0 14.9 %pull.4 = (bf16[128,2048]{1,0:T(8,128)(2,1)S(1)}, bf16[128,2048]{1,0:T(8,128)(2,1)S(1)}, bf16[128,2048]{1,0:T(8,128)(2,1)S(1)}, bf16[128,2048]{1,0:T(8,128)(2,1)}, f32[8,128]{1,0:T(8,128)S(1)}, /*index=5*/f32[1,1]{1,0:T(1,128)}) custom-call(f32[8,128]{1,0:T(8,128)S(1)} %get-tuple-element.108.refs_0_, ...), custom_call_target="tpu_custom_call" | custom-call | flops 5800000000 | bytes 1 | tf_op jit(solution)/shard_map/pull/pallas_call | solution.py:97
  171.4 10.9 %ffn_back.3 = (bf16[512,2048]{1,0:T(8,128)(2,1)}, bf16[512,2048]{1,0:T(8,128)(2,1)}, f32[8,128]{1,0:T(8,128)S(1)}) custom-call(s32[4]{0:T(128)S(1)} %iota_xor_fusion.1.refs_2_.refs_0_.refs_3_.refs_1_, f32[8,128]{1,0:T(8,128)S(1)} %get-tuple-element.116.refs_1_, ...), custom_call_target="tpu_custom_call" | custom-call | flops 5800000000 | bytes 1 | tf_op jit(solution)/shard_map/ffn_back/pallas_call | solution.py:97
  183.1 6.8 %weight_terms.9 = (bf16[512,2048]{1,0:T(8,128)(2,1)}, f32[8,128]{1,0:T(8,128)S(1)}) custom-call(s32[2]{0:T(128)S(1)} %add_add_fusion.5.refs_0_.refs_1_, s32[2]{0:T(128)S(1)} %add_add_fusion.5.refs_0_.refs_1_, s32[4]{0:T(128)S(1)} %iota_xor_fusion.1.refs_2_.refs_0_.refs_3_.refs_1_, bf16[128,2048]{1,0:T(8,128)(2,1)S(1)} %add_convert_fusion.2.refs_3_, ...), custom_call_target="tpu_custom_call" | custom-call | flops 5800000000 | bytes 1 | tf_op jit(solution)/shard_map/weight_terms/pallas_call | solution.py:97
  193.0 7.8 %weight_terms.10 = (bf16[256,2048]{1,0:T(8,128)(2,1)}, bf16[256,2048]{1,0:T(8,128)(2,1)}, f32[8,128]{1,0:T(8,128)S(1)}, f32[1,1]{1,0:T(1,128)}) custom-call(s32[2]{0:T(128)S(1)} %and_select_fusion.1.refs_0_, s32[2]{0:T(128)S(1)} %gather_fusion, s32[2]{0:T(128)S(1)} %gather_fusion, s32[4]{0:T(128)S(1)} %iota_xor_fusion.1.refs_2_.refs_0_.refs_3_.refs_1_, ...), custom_call_target="tpu_custom_call" | custom-call | flops 5800000000 | bytes 1 | tf_op jit(solution)/shard_map/weight_terms/pallas_call | solution.py:97
  205.2 9.5 %collective-permute-start.29 = (bf16[256,2048]{1,0:T(8,128)(2,1)}, bf16[256,2048]{1,0:T(8,128)(2,1)S(1)}, u32[]{:S(2)}, u32[]{:S(2)}) collective-permute-start(bf16[256,2048]{1,0:T(8,128)(2,1)} %get-tuple-element.132), channel_id=1, source_target_pairs={{0,8},{4,12},{8,0},{12,4},{1,9},{5,13},{9,1},{13,5},{2,10},{6,14},... | collective-permute-start | bytes 3145736 | tf_op jit(solution)/shard_map/ppermute | solution.py:743
  214.6 6.8 %weight_terms.11 = (bf16[512,2048]{1,0:T(8,128)(2,1)}, f32[8,128]{1,0:T(8,128)S(1)}) custom-call(s32[2]{0:T(128)S(1)} %add_add_fusion.5.refs_0_.refs_1_, s32[2]{0:T(128)S(1)} %add_add_fusion.5.refs_0_.refs_1_, s32[4]{0:T(128)S(1)} %iota_xor_fusion.1.refs_2_.refs_0_.refs_3_.refs_1_, bf16[128,2048]{1,0:T(8,128)(2,1)S(1)} %get-tuple-element.208.refs_3_.refs_8_.refs_5_, ...), custom_call_target="tpu_custom_call" | custom-call | flops 5800000000 | bytes 1 | tf_op jit(solution)/shard_map/weight_terms/pallas_call | solution.py:97
  228.2 15.4 %attend_back.1 = (bf16[512,512]{1,0:T(8,128)(2,1)}, f32[512,256]{1,0:T(8,128)}, bf16[512,256]{1,0:T(8,128)(2,1)S(1)}, bf16[256,256]{1,0:T(8,128)(2,1)S(1)}, bf16...) custom-call(f32[8,128]{1,0:T(8,128)S(1)} %get-tuple-element.126.refs_0_, s32[16]{0:T(128)S(1)} %concatenate.33.refs_4_.refs_1_, ...), custom_call_target="tpu_custom_call" | custom-call | flops 5800000000 | bytes 1 | tf_op jit(solution)/shard_map/attend_back/pallas_call | solution.py:97
  243.6 16.4 %collective-permute-start.26 = (bf16[256,256]{1,0:T(8,128)(2,1)S(1)}, bf16[256,256]{1,0:T(8,128)(2,1)S(1)}, u32[]{:S(2)}, u32[]{:S(2)}) collective-permute-start(bf16[256,256]{1,0:T(8,128)(2,1)S(1)} %get-tuple-element.129), channel_id=1, source_target_pairs={{0,8},{8,0},{12,4},{1,9},{9,1},{13,5},{2,10},{10,2},{14,6},{3,11},... | collective-permute-start | bytes 393224 | tf_op jit(solution)/shard_map/ppermute | solution.py:992
  264.1 7.3 %weight_terms.12 = (bf16[256,2048]{1,0:T(8,128)(2,1)}, bf16[256,2048]{1,0:T(8,128)(2,1)S(1)}, f32[8,128]{1,0:T(8,128)S(1)}, f32[1,1]{1,0:T(1,128)}) custom-call(s32[2]{0:T(128)S(1)} %and_select_fusion.1.refs_0_, s32[2]{0:T(128)S(1)} %gather_fusion, s32[2]{0:T(128)S(1)} %gather_fusion, s32[4]{0:T(128)S(1)} %iota_xor_fusion.1.refs_2_.refs_0_.refs_3_.refs_1_, ...), custom_call_target="tpu_custom_call" | custom-call | flops 5800000000 | bytes 1 | tf_op jit(solution)/shard_map/weight_terms/pallas_call | solution.py:97
  277.6 4.9 %collective-permute-done.21.refs_4_.refs_16_ = bf16[512,2048]{1,0:T(8,128)(2,1)} collective-permute-done((bf16[512,2048]{1,0:T(8,128)(2,1)}, bf16[512,2048]{1,0:T(8,128)(2,1)}, u32[]{:S(2)}, u32[]{:S(2)}) %collective-permute-start.21) | collective-permute-done | bytes 2097184 | tf_op jit(solution)/shard_map/ppermute | solution.py:743
  282.4 7.2 %weight_terms.13 = (bf16[256,2048]{1,0:T(8,128)(2,1)}, bf16[256,2048]{1,0:T(8,128)(2,1)S(1)}, f32[8,128]{1,0:T(8,128)S(1)}, f32[1,1]{1,0:T(1,128)}) custom-call(s32[2]{0:T(128)S(1)} %and_select_fusion.1.refs_0_, s32[2]{0:T(128)S(1)} %gather_fusion, s32[2]{0:T(128)S(1)} %gather_fusion, s32[4]{0:T(128)S(1)} %iota_xor_fusion.1.refs_2_.refs_0_.refs_3_.refs_1_, ...), custom_call_target="tpu_custom_call" | custom-call | flops 5800000000 | bytes 1 | tf_op jit(solution)/shard_map/weight_terms/pallas_call | solution.py:97
  290.7 4.8 %own_terms.2 = (bf16[1024,512]{1,0:T(8,128)(2,1)}, f32[8,128]{1,0:T(8,128)S(1)}, f32[1,1]{1,0:T(1,128)}) custom-call(s32[4]{0:T(128)S(1)} %fusion.21.refs_0_, s32[4]{0:T(128)S(1)} %iota_xor_fusion.1.refs_2_.refs_0_.refs_3_.refs_1_, f32[8,128]{1,0:T(8,128)S(1)} %get-tuple-element.138.refs_2_, bf16[128,2048]{1,0:T(8,128)(2,1)S(1)} %copy-done.26, ...), custom_call_target="tpu_custom_call" | custom-call | flops 5800000000 | bytes 1 | tf_op jit(solution)/shard_map/own_terms/pallas_call | solution.py:97
  297.1 9.5 %collective-permute-start.40 = (bf16[256,2048]{1,0:T(8,128)(2,1)}, bf16[256,2048]{1,0:T(8,128)(2,1)}, u32[]{:S(2)}, u32[]{:S(2)}) collective-permute-start(bf16[256,2048]{1,0:T(8,128)(2,1)} %get-tuple-element.158), channel_id=1, source_target_pairs={{0,8},{4,12},{8,0},{12,4},{1,9},{5,13},{9,1},{13,5},{2,10},{6,14},... | collective-permute-start | bytes 3145736 | tf_op jit(solution)/shard_map/ppermute | solution.py:743
  309.9 7.7 %push.1 = (bf16[512,2048]{1,0:T(8,128)(2,1)S(1)}, f32[8,128]{1,0:T(8,128)S(1)}) custom-call(s32[4]{0:T(128)S(1)} %iota_xor_fusion.1.refs_2_.refs_0_.refs_3_.refs_1_, f32[8,128]{1,0:T(8,128)S(1)} %get-tuple-element.142.refs_1_, bf16[512,2048]{1,0:T(8,128)(2,1)S(1)} %copy-done, bf16[2048,2048]{1,0:T(8,128)(2,1)} %refs_3_.3), custom_call_target="tpu_custom_call" | custom-call | flops 5800000000 | bytes 1 | tf_op jit(solution)/shard_map/push/pallas_call | solution.py:97
  334.0 12.5 %collective-permute-done.35.refs_4_.refs_17_ = bf16[512,768]{1,0:T(8,128)(2,1)} collective-permute-done((bf16[512,768]{1,0:T(8,128)(2,1)}, bf16[512,768]{1,0:T(8,128)(2,1)}, u32[]{:S(2)}, u32[]{:S(2)}) %collective-permute-start.35) | collective-permute-done | bytes 786464 | tf_op jit(solution)/shard_map/ppermute | solution.py:743
  394.5 11.2 %collective-permute-done.45 = bf16[256,512]{1,0:T(8,128)(2,1)S(1)} collective-permute-done((bf16[256,512]{1,0:T(8,128)(2,1)S(1)}, bf16[256,512]{1,0:T(8,128)(2,1)S(1)}, u32[]{:S(2)}, u32[]{:S(2)}) %collective-permute-start.45) | collective-permute-done | bytes 262176 | tf_op jit(solution)/shard_map/ppermute | solution.py:743
  (321 shorter events, 154.0 us)
Async XLA Ops:
  7.2 129.7 %all-gather.2.cloned.1.call-start = ((), (), s32[]{:S(2)}) async-start(), calls=%async_computation.1 | async-start | bytes 6553600 | tf_op jit(solution)/shard_map/all_gather | solution.py:942
  12.0 20.9 %collective-permute-start.16 = (bf16[128,3072]{1,0:T(8,128)(2,1)}, bf16[128,3072]{1,0:T(8,128)(2,1)}, u32[]{:S(2)}, u32[]{:S(2)}) collective-permute-start(bf16[128,3072]{1,0:T(8,128)(2,1)} %pad_maximum_fusion.1), channel_id=1, source_target_pairs={{0,4},{4,0},{8,12},{12,8},{1,5},{5,1},{9,13},{13,9},{2,6},{6,2},{1... | collective-permute-start | bytes 2359304 | tf_op jit(solution)/shard_map/ppermute | solution.py:743
  16.6 18.9 %collective-permute-start = (bf16[128,2048]{1,0:T(8,128)(2,1)S(1)}, bf16[128,2048]{1,0:T(8,128)(2,1)S(1)}, u32[]{:S(2)}, u32[]{:S(2)}) collective-permute-start(bf16[128,2048]{1,0:T(8,128)(2,1)S(1)} %fusion.2.refs_0_.refs_5_.refs_7_), channel_id=1, source_target_pairs={{0,1},{1,0},{2,3},{3,2},{4,5},{5,4},{6,7},{7,6},{8,9},{9,8},{10,11... | collective-permute-start | bytes 1572872 | tf_op jit(solution)/shard_map/ppermute | solution.py:743
  35.5 336.5 %reduce-scatter.2.cloned.1.call-start = ((), (), s32[]{:S(2)}) async-start(), calls=%async_computation.2 | async-start | bytes 2621440 | tf_op jit(solution)/shard_map/reduce_scatter | solution.py:1005
  68.7 18.4 %collective-permute-start.8 = (bf16[128,2048]{1,0:T(8,128)(2,1)S(1)}, bf16[128,2048]{1,0:T(8,128)(2,1)S(1)}, u32[]{:S(2)}, u32[]{:S(2)}) collective-permute-start(bf16[128,2048]{1,0:T(8,128)(2,1)S(1)} %add_convert_fusion.4), channel_id=1, source_target_pairs={{0,2},{1,3},{2,0},{3,1},{4,6},{5,7},{6,4},{7,5},{8,10},{9,11},{10,... | collective-permute-start | bytes 1572872 | tf_op jit(solution)/shard_map/ppermute | solution.py:743
  101.5 16.3 %collective-permute-start.14 = (bf16[128,2048]{1,0:T(8,128)(2,1)S(1)}, bf16[128,2048]{1,0:T(8,128)(2,1)S(1)}, u32[]{:S(2)}, u32[]{:S(2)}) collective-permute-start(bf16[128,2048]{1,0:T(8,128)(2,1)S(1)} %collective-permute-done.12.refs_1_.refs_9_.refs_11_.refs_10_), channel_id=1, source_target_pairs={{0,2},{1,3},{2,0},{3,1},{4,6},{5,7},{6,4},{7,5},{8,10},{9,11},{10,... | collective-permute-start | bytes 1572872 | tf_op jit(solution)/shard_map/ppermute | solution.py:743
  103.2 17.2 %collective-permute-start.13 = (bf16[128,2048]{1,0:T(8,128)(2,1)S(1)}, bf16[128,2048]{1,0:T(8,128)(2,1)}, u32[]{:S(2)}, u32[]{:S(2)}) collective-permute-start(bf16[128,2048]{1,0:T(8,128)(2,1)S(1)} %collective-permute-done.12.refs_1_.refs_9_.refs_11_.refs_10_), channel_id=1, source_target_pairs={{0,1},{1,0},{2,3},{3,2},{4,5},{5,4},{6,7},{7,6},{8,9},{9,8},{10,11... | collective-permute-start | bytes 1572872 | tf_op jit(solution)/shard_map/ppermute | solution.py:743
  143.7 48.0 %collective-permute-start.20 = (bf16[512,2048]{1,0:T(8,128)(2,1)}, bf16[512,2048]{1,0:T(8,128)(2,1)S(1)}, u32[]{:S(2)}, u32[]{:S(2)}) collective-permute-start(bf16[512,2048]{1,0:T(8,128)(2,1)} %get-tuple-element.115), channel_id=1, source_target_pairs={{0,16},{16,0},{1,17},{17,1},{2,18},{18,2},{3,19},{19,3},{4,20},{20... | collective-permute-start | bytes 6291464 | tf_op jit(solution)/shard_map/ppermute | solution.py:743
  170.9 29.9 %collective-permute-start.17 = (bf16[128,2048]{1,0:T(8,128)(2,1)S(1)}, bf16[128,2048]{1,0:T(8,128)(2,1)S(1)}, u32[]{:S(2)}, u32[]{:S(2)}) collective-permute-start(bf16[128,2048]{1,0:T(8,128)(2,1)S(1)} %get-tuple-element.112), channel_id=1, source_target_pairs={{0,1},{1,0},{2,3},{3,2},{4,5},{5,4},{6,7},{7,6},{8,9},{9,8},{10,11... | collective-permute-start | bytes 1572872 | tf_op jit(solution)/shard_map/ppermute | solution.py:743
  182.5 18.3 %collective-permute-start.19 = (bf16[128,2048]{1,0:T(8,128)(2,1)S(1)}, bf16[128,2048]{1,0:T(8,128)(2,1)S(1)}, u32[]{:S(2)}, u32[]{:S(2)}) collective-permute-start(bf16[128,2048]{1,0:T(8,128)(2,1)S(1)} %add_convert_fusion.2.refs_3_), channel_id=1, source_target_pairs={{0,2},{1,3},{2,0},{3,1},{4,6},{5,7},{6,4},{7,5},{8,10},{9,11},{10,... | collective-permute-start | bytes 1572872 | tf_op jit(solution)/shard_map/ppermute | solution.py:743
  189.9 71.4 %collective-permute-start.28 = (bf16[512,2048]{1,0:T(8,128)(2,1)}, bf16[512,2048]{1,0:T(8,128)(2,1)}, u32[]{:S(2)}, u32[]{:S(2)}) collective-permute-start(bf16[512,2048]{1,0:T(8,128)(2,1)} %get-tuple-element.131), channel_id=1, source_target_pairs={{0,16},{16,0},{1,17},{17,1},{2,18},{18,2},{3,19},{19,3},{4,20},{20... | collective-permute-start | bytes 6291464 | tf_op jit(solution)/shard_map/ppermute | solution.py:743
  204.7 18.4 %collective-permute-start.23 = (bf16[128,2048]{1,0:T(8,128)(2,1)S(1)}, bf16[128,2048]{1,0:T(8,128)(2,1)}, u32[]{:S(2)}, u32[]{:S(2)}) collective-permute-start(bf16[128,2048]{1,0:T(8,128)(2,1)S(1)} %get-tuple-element.208.refs_3_.refs_8_.refs_5_), channel_id=1, source_target_pairs={{0,2},{1,3},{2,0},{3,1},{4,6},{5,7},{6,4},{7,5},{8,10},{9,11},{10,... | collective-permute-start | bytes 1572872 | tf_op jit(solution)/shard_map/ppermute | solution.py:743
  205.2 20.0 %collective-permute-start.22 = (bf16[128,2048]{1,0:T(8,128)(2,1)S(1)}, bf16[128,2048]{1,0:T(8,128)(2,1)}, u32[]{:S(2)}, u32[]{:S(2)}) collective-permute-start(bf16[128,2048]{1,0:T(8,128)(2,1)S(1)} %get-tuple-element.208.refs_3_.refs_8_.refs_5_), channel_id=1, source_target_pairs={{0,1},{1,0},{2,3},{3,2},{4,5},{5,4},{6,7},{7,6},{8,9},{9,8},{10,11... | collective-permute-start | bytes 1572872 | tf_op jit(solution)/shard_map/ppermute | solution.py:743
  205.2 58.8 %collective-permute-start.29 = (bf16[256,2048]{1,0:T(8,128)(2,1)}, bf16[256,2048]{1,0:T(8,128)(2,1)S(1)}, u32[]{:S(2)}, u32[]{:S(2)}) collective-permute-start(bf16[256,2048]{1,0:T(8,128)(2,1)} %get-tuple-element.132), channel_id=1, source_target_pairs={{0,8},{4,12},{8,0},{12,4},{1,9},{5,13},{9,1},{13,5},{2,10},{6,14},... | collective-permute-start | bytes 3145736 | tf_op jit(solution)/shard_map/ppermute | solution.py:743
  221.4 61.0 %collective-permute-start.21 = (bf16[512,2048]{1,0:T(8,128)(2,1)}, bf16[512,2048]{1,0:T(8,128)(2,1)}, u32[]{:S(2)}, u32[]{:S(2)}) collective-permute-start(bf16[512,2048]{1,0:T(8,128)(2,1)} %get-tuple-element.125), channel_id=1, source_target_pairs={{0,16},{16,0},{1,17},{17,1},{2,18},{18,2},{3,19},{19,3},{4,20},{20... | collective-permute-start | bytes 6291464 | tf_op jit(solution)/shard_map/ppermute | solution.py:743
  243.6 28.8 %collective-permute-start.26 = (bf16[256,256]{1,0:T(8,128)(2,1)S(1)}, bf16[256,256]{1,0:T(8,128)(2,1)S(1)}, u32[]{:S(2)}, u32[]{:S(2)}) collective-permute-start(bf16[256,256]{1,0:T(8,128)(2,1)S(1)} %get-tuple-element.129), channel_id=1, source_target_pairs={{0,8},{8,0},{12,4},{1,9},{9,1},{13,5},{2,10},{10,2},{14,6},{3,11},... | collective-permute-start | bytes 393224 | tf_op jit(solution)/shard_map/ppermute | solution.py:992
  272.4 61.2 %collective-permute-start.36 = (bf16[256,2048]{1,0:T(8,128)(2,1)}, bf16[256,2048]{1,0:T(8,128)(2,1)S(1)}, u32[]{:S(2)}, u32[]{:S(2)}) collective-permute-start(bf16[256,2048]{1,0:T(8,128)(2,1)} %get-tuple-element.153), channel_id=1, source_target_pairs={{0,8},{4,12},{8,0},{12,4},{1,9},{5,13},{9,1},{13,5},{2,10},{6,14},... | collective-permute-start | bytes 3145736 | tf_op jit(solution)/shard_map/ppermute | solution.py:743
  276.1 42.9 %collective-permute-start.33 = (bf16[512,768]{1,0:T(8,128)(2,1)S(1)}, bf16[512,768]{1,0:T(8,128)(2,1)S(1)}, u32[]{:S(2)}, u32[]{:S(2)}) collective-permute-start(bf16[512,768]{1,0:T(8,128)(2,1)S(1)} %get-tuple-element.148.refs_13_.refs_15_), channel_id=1, source_target_pairs={{0,4},{4,0},{8,12},{12,8},{1,5},{5,1},{9,13},{13,9},{2,6},{6,2},{1... | collective-permute-start | bytes 2359304 | tf_op jit(solution)/shard_map/ppermute | solution.py:743
  295.5 62.9 %collective-permute-start.34 = (bf16[1024,512]{1,0:T(8,128)(2,1)}, bf16[1024,512]{1,0:T(8,128)(2,1)}, u32[]{:S(2)}, u32[]{:S(2)}) collective-permute-start(bf16[1024,512]{1,0:T(8,128)(2,1)} %get-tuple-element.151), channel_id=1, source_target_pairs={{0,4},{4,0},{8,12},{12,8},{1,5},{5,1},{9,13},{13,9},{2,6},{6,2},{1... | collective-permute-start | bytes 3145736 | tf_op jit(solution)/shard_map/ppermute | solution.py:743
  297.1 76.7 %collective-permute-start.40 = (bf16[256,2048]{1,0:T(8,128)(2,1)}, bf16[256,2048]{1,0:T(8,128)(2,1)}, u32[]{:S(2)}, u32[]{:S(2)}) collective-permute-start(bf16[256,2048]{1,0:T(8,128)(2,1)} %get-tuple-element.158), channel_id=1, source_target_pairs={{0,8},{4,12},{8,0},{12,4},{1,9},{5,13},{9,1},{13,5},{2,10},{6,14},... | collective-permute-start | bytes 3145736 | tf_op jit(solution)/shard_map/ppermute | solution.py:743
  326.3 20.1 %collective-permute-start.35 = (bf16[512,768]{1,0:T(8,128)(2,1)}, bf16[512,768]{1,0:T(8,128)(2,1)}, u32[]{:S(2)}, u32[]{:S(2)}) collective-permute-start(bf16[512,768]{1,0:T(8,128)(2,1)} %get-tuple-element.152), channel_id=1, source_target_pairs={{0,16},{16,0},{1,17},{17,1},{2,18},{18,2},{3,19},{19,3},{4,20},{20... | collective-permute-start | bytes 2359304 | tf_op jit(solution)/shard_map/ppermute | solution.py:743
  331.7 22.6 %collective-permute-start.30 = (bf16[128,2048]{1,0:T(8,128)(2,1)}, bf16[128,2048]{1,0:T(8,128)(2,1)S(1)}, u32[]{:S(2)}, u32[]{:S(2)}) collective-permute-start(bf16[128,2048]{1,0:T(8,128)(2,1)} %copy-done.44), channel_id=1, source_target_pairs={{0,1},{1,0},{2,3},{3,2},{4,5},{5,4},{6,7},{7,6},{8,9},{9,8},{10,11... | collective-permute-start | bytes 1572872 | tf_op jit(solution)/shard_map/ppermute | solution.py:743
  333.6 23.5 %collective-permute-start.32 = (bf16[128,2048]{1,0:T(8,128)(2,1)S(1)}, bf16[128,2048]{1,0:T(8,128)(2,1)S(1)}, u32[]{:S(2)}, u32[]{:S(2)}) collective-permute-start(bf16[128,2048]{1,0:T(8,128)(2,1)S(1)} %add_convert_fusion), channel_id=1, source_target_pairs={{0,2},{1,3},{2,0},{3,1},{4,6},{5,7},{6,4},{7,5},{8,10},{9,11},{10,... | collective-permute-start | bytes 1572872 | tf_op jit(solution)/shard_map/ppermute | solution.py:743
  354.2 32.4 %collective-permute-start.44 = (bf16[256,768]{1,0:T(8,128)(2,1)}, bf16[256,768]{1,0:T(8,128)(2,1)}, u32[]{:S(2)}, u32[]{:S(2)}) collective-permute-start(bf16[256,768]{1,0:T(8,128)(2,1)} %get-tuple-element.163), channel_id=1, source_target_pairs={{0,8},{4,12},{8,0},{12,4},{1,9},{5,13},{9,1},{13,5},{2,10},{6,14},... | collective-permute-start | bytes 1179656 | tf_op jit(solution)/shard_map/ppermute | solution.py:743
  (106 other events, 1054.9 us)
Sparse Core Ops, SparseCore 0:
  35.6 46.1 all-gather.1
  319.1 37.3 reduce-scatter.1
